TPU v7x, 32 devices: a whole 2x2x4 slice. The times are simulated.
32 devices in a mesh: head: 4 (over x, core), ctx: 8 (over z, y).
Axes of the slice: x: 2, y: 2, z: 4, core: 2. Of those that a mesh axis runs over, the one named last changes fastest.
Arguments:
- queries: bfloat16 [16, 4096, 128], P(None, ('ctx', 'head')), may hold values from -6 to 6
- key_rows: bfloat16 [4096, 128], P(('ctx', 'head')), may hold values from -6 to 6
- value_rows: bfloat16 [4096, 128], P(('ctx', 'head')), may hold values from -6 to 6
- attn_output: bfloat16 [16, 4096, 128], P(None, ('ctx', 'head')), may hold values from -6 to 6
- grad_output: bfloat16 [16, 4096, 128], P(None, ('ctx', 'head')), may hold values from -6 to 6
- logsumexp: float32 [16, 4096], P(None, ('ctx', 'head')), as said below
- positions: int32 [4096], P(('ctx', 'head')), may hold values from 0 to 4095, as said below
Outputs:
- grad_queries: bfloat16 [16, 4096, 128], P(None, ('ctx', 'head'))
- grad_keys: bfloat16 [4096, 128], P(('ctx', 'head'))
- grad_values: bfloat16 [4096, 128], P(('ctx', 'head'))
Inputs may be any that keep to these rules, and one draw needn't show every extreme that they name: positions is a permutation of 0 to 4095. The sequence is cut into 16 runs of 256 consecutive positions; the 512 tokens of each index of ctx are, in order, one run r and then run 2 * 8 - 1 - r, each in increasing order; which r falls on which index is drawn. logsumexp[h, i] lies between log(positions[i] + 1) + 0.2 and log(positions[i] + 1) + 1.2.
All inputs are finite; a program needn't handle non-finite values.
Results may differ from a plain program's by a relative error of at most 0.0055.
Values may be sent and summed in bfloat16 or wider, within the bound.
A program may use at most 64 MiB of HBM per device.

v0:
```python
from functools import partial

import jax
import jax.numpy as jnp
from jax import lax
from jax.sharding import PartitionSpec as P


def from_behind(block, axis, distance):
    devices = range(lax.axis_size(axis))
    route = [((i - distance) % len(devices), i) for i in devices]
    return lax.ppermute(block, axis, route)


def tile_terms(
    scaling, query_run, grad_run, lse_run, delta_run, query_at, key_run, value_run, key_at
):
    scores = (
        jnp.einsum("hqd,kd->hqk", query_run, key_run, preferred_element_type=jnp.float32) * scaling
    )
    visible = key_at[None, None, :] <= query_at[None, :, None]
    attention = jnp.where(visible, jnp.exp(scores - lse_run[:, :, None]), 0.0)
    attention_low = attention.astype(jnp.bfloat16)
    grad_probs = jnp.einsum("hqd,kd->hqk", grad_run, value_run, preferred_element_type=jnp.float32)
    grad_scores = (attention * (grad_probs - delta_run[:, :, None])).astype(jnp.bfloat16)
    query_grad = jnp.einsum("hqk,kd->hqd", grad_scores, key_run, preferred_element_type=jnp.float32)
    key_grad = jnp.einsum("hqk,hqd->kd", grad_scores, query_run, preferred_element_type=jnp.float32)
    value_grad = jnp.einsum(
        "hqk,hqd->kd", attention_low, grad_run, preferred_element_type=jnp.float32
    )
    return (query_grad, key_grad, value_grad)


def local(queries, key_rows, value_rows, attn_output, grad_output, logsumexp, positions):
    scaling = queries.shape[2] ** (-0.5)
    width = queries.shape[2]
    cycle_size = lax.axis_size("ctx")
    group_size = lax.axis_size("head")
    local_rows = positions.shape[0]
    ctx_rows = local_rows * group_size
    run_rows = ctx_rows // 2
    query_rows, output_rows, grad_rows = (
        lax.all_to_all(queries, "head", split_axis=0, concat_axis=1, tiled=True),
        lax.all_to_all(attn_output, "head", split_axis=0, concat_axis=1, tiled=True),
        lax.all_to_all(grad_output, "head", split_axis=0, concat_axis=1, tiled=True),
    )
    lse_rows = lax.all_to_all(logsumexp, "head", split_axis=0, concat_axis=1, tiled=True)
    row_delta = jnp.sum(grad_rows.astype(jnp.float32) * output_rows.astype(jnp.float32), axis=2)
    key_block, value_block = (
        lax.all_gather(key_rows, "head", axis=0, tiled=True),
        lax.all_gather(value_rows, "head", axis=0, tiled=True),
    )
    all_places = lax.all_gather(positions, ("head", "ctx"), axis=0, tiled=True)
    all_places = (
        all_places.reshape(group_size, cycle_size, local_rows)
        .transpose(1, 0, 2)
        .reshape(cycle_size, ctx_rows)
    )
    cycle_index = lax.axis_index("ctx")
    query_places = lax.dynamic_index_in_dim(all_places, cycle_index, 0, keepdims=False)
    head_count = query_rows.shape[0]
    nothing = (
        jnp.zeros((head_count, run_rows, width), jnp.float32),
        jnp.zeros((run_rows, width), jnp.float32),
        jnp.zeros((run_rows, width), jnp.float32),
    )

    def block_terms(key_now, value_now, key_places):
        query_parts = []
        key_parts = [nothing[1], nothing[1]]
        value_parts = [nothing[2], nothing[2]]
        for query_half in range(2):
            row_from = query_half * run_rows
            query_run = query_rows[:, row_from : row_from + run_rows]
            grad_run = grad_rows[:, row_from : row_from + run_rows]
            lse_run = lse_rows[:, row_from : row_from + run_rows]
            delta_run = row_delta[:, row_from : row_from + run_rows]
            query_at = query_places[row_from : row_from + run_rows]
            query_total = nothing[0]
            for key_half in range(2):
                key_from = key_half * run_rows
                key_at = key_places[key_from : key_from + run_rows]
                worker = partial(
                    tile_terms,
                    scaling,
                    query_run,
                    grad_run,
                    lse_run,
                    delta_run,
                    query_at,
                    key_now[key_from : key_from + run_rows],
                    value_now[key_from : key_from + run_rows],
                    key_at,
                )
                visible = jnp.max(query_at) >= jnp.min(key_at)
                query_grad, key_grad, value_grad = lax.cond(visible, worker, lambda: nothing)
                query_total = query_total + query_grad
                key_parts[key_half] = key_parts[key_half] + key_grad
                value_parts[key_half] = value_parts[key_half] + value_grad
            query_parts.append(query_total)
        return (
            jnp.concatenate(query_parts, axis=1),
            jnp.concatenate(key_parts, axis=0),
            jnp.concatenate(value_parts, axis=0),
        )

    def places_of(offset):
        source = (cycle_index - offset) % cycle_size
        return (source, lax.dynamic_index_in_dim(all_places, source, 0, keepdims=False))

    rounds = cycle_size - 1
    query_start = jnp.zeros(query_rows.shape, jnp.float32)

    def advance(offset, carried):
        key_now, value_now, key_acc, value_acc, query_acc = carried
        source, key_places = places_of(offset)
        query_grad, key_grad, value_grad = block_terms(key_now, value_now, key_places)
        key_acc, value_acc = from_behind((key_acc + key_grad, value_acc + value_grad), "ctx", 1)
        key_now, value_now = from_behind((key_now, value_now), "ctx", 1)
        return (key_now, value_now, key_acc, value_acc, query_acc + query_grad)

    zero_rows = jnp.zeros((ctx_rows, width), jnp.float32)
    carried = lax.fori_loop(
        0, rounds, advance, (key_block, value_block, zero_rows, zero_rows, query_start)
    )
    key_now, value_now, key_acc, value_acc, query_acc = carried
    source, key_places = places_of(rounds)
    query_grad, key_grad, value_grad = block_terms(key_now, value_now, key_places)
    query_acc = query_acc + query_grad
    key_sums, value_sums = from_behind((key_acc + key_grad, value_acc + value_grad), "ctx", 1)
    key_mine, value_mine = (
        lax.psum_scatter(key_sums, "head", scatter_dimension=0, tiled=True),
        lax.psum_scatter(value_sums, "head", scatter_dimension=0, tiled=True),
    )
    grad_keys = (key_mine * scaling).astype(jnp.bfloat16)
    grad_values = value_mine.astype(jnp.bfloat16)
    query_low = (query_acc * scaling).astype(jnp.bfloat16)
    grad_queries = lax.all_to_all(query_low, "head", split_axis=1, concat_axis=0, tiled=True)
    return (grad_queries, grad_keys, grad_values)


def solution(mesh):
    return jax.shard_map(
        local,
        mesh=mesh,
        in_specs=(
            P(None, ("ctx", "head"), None),
            P(("ctx", "head"), None),
            P(("ctx", "head"), None),
            P(None, ("ctx", "head"), None),
            P(None, ("ctx", "head"), None),
            P(None, ("ctx", "head")),
            P(("ctx", "head")),
        ),
        out_specs=(
            P(None, ("ctx", "head"), None),
            P(("ctx", "head"), None),
            P(("ctx", "head"), None),
        ),
        check_vma=False,
    )
```

profile of v0, /device:TPU:0, one launch (start us, length us, event | category | flops | bytes accessed | tf_op | source)
XLA Modules:
  0.0 501.0 jit_solution(16597341178051399940)
XLA Ops:
  7.2 8.0 %all_to_all.82 = f32[4,4,128]{2,1,0:T(4,128)S(1)} all-to-all(f32[4,4,128]{2,1,0:T(4,128)} %bitcast.210), channel_id=1, replica_groups=mesh['head'=4,'ctx'=8] {'head'}, dimensions={0} | all-to-all | bytes 16384 | tf_op jit(solution)/shard_map/all_to_all | solution.py:47
  15.2 12.3 %all_to_all.83 = bf16[16,128,128]{2,1,0:T(8,128)(2,1)S(1)} all-to-all(bf16[16,128,128]{2,1,0:T(8,128)(2,1)} %param.25), channel_id=1, replica_groups=mesh['head'=4,'ctx'=8] {'head'}, dimensions={0} | all-to-all | bytes 1048576 | tf_op jit(solution)/shard_map/all_to_all | solution.py:43
  27.5 3.5 all-to-all-start.2
  31.6 71.4 %all-gather = s32[32,1,128]{2,1,0:T(1,128)} all-gather(s32[1,1,128]{2,1,0:T(1,128)S(1)} %bitcast.211), channel_id=1, replica_groups=mesh['head'=4,'ctx'=8] {'head','ctx'}, dimensions={0}, use_global_device_ids=true | all-gather | bytes 16896 | tf_op jit(solution)/shard_map/all_gather | solution.py:53
  103.1 2.2 fusion.85
  105.3 3.6 all-to-all-start.3
  108.9 10.7 %all_gather.9 = bf16[512,128]{1,0:T(8,128)(2,1)} all-gather(bf16[128,128]{1,0:T(8,128)(2,1)S(1)} %copy-done.48), channel_id=1, replica_groups=mesh['head'=4,'ctx'=8] {'head'}, dimensions={0}, use_global_device_ids=true | all-gather | bytes 163840 | tf_op jit(solution)/shard_map/all_gather | solution.py:50
  124.8 5.9 %all_gather.10 = bf16[512,128]{1,0:T(8,128)(2,1)} all-gather(bf16[128,128]{1,0:T(8,128)(2,1)S(1)} %copy-done.49), channel_id=1, replica_groups=mesh['head'=4,'ctx'=8] {'head'}, dimensions={0}, use_global_device_ids=true | all-gather | bytes 163840 | tf_op jit(solution)/shard_map/all_gather | solution.py:51
  136.0 2.2 fusion.96
  139.7 285.2 %while.24 = (s32[]{:T(128)}, bf16[512,128]{1,0:T(8,128)(2,1)}, bf16[512,128]{1,0:T(8,128)(2,1)}, f32[512,128]{1,0:T(8,128)}, f32[512,128]{1,0:T(8,128)}, /*index...) while((s32[]{:T(128)}, bf16[512,128]{1,0:T(8,128)(2,1)}, ...), condition=%wide.region_14.15_spmd.clone, body=%wide.region_3.14_spmd.clone.sunk | while | flops 1351221760 | bytes 47113660 | solution.py:123
  143.3 2.0 fusion.155
  159.0 3.0 conditional.23
  170.1 8.4 %collective-permute-done.3 = f32[512,128]{1,0:T(8,128)} collective-permute-done((f32[512,128]{1,0:T(8,128)S(1)}, f32[512,128]{1,0:T(8,128)}, u32[]{:S(2)}, u32[]{:S(2)}) %collective-permute-start.3) | collective-permute-done | bytes 262176 | tf_op jit(solution)/shard_map/while/body/eval_jaxpr/ppermute | solution.py:12
  178.5 4.5 collective-permute-done.2
  186.8 2.0 fusion.155
  200.7 3.0 conditional.23
  213.3 7.0 %collective-permute-done.3 = f32[512,128]{1,0:T(8,128)} collective-permute-done((f32[512,128]{1,0:T(8,128)S(1)}, f32[512,128]{1,0:T(8,128)}, u32[]{:S(2)}, u32[]{:S(2)}) %collective-permute-start.3) | collective-permute-done | bytes 262176 | tf_op jit(solution)/shard_map/while/body/eval_jaxpr/ppermute | solution.py:12
  220.3 3.6 collective-permute-done.2
  227.6 2.0 fusion.155
  241.6 3.0 conditional.23
  249.0 2.7 collective-permute-start.3
  254.3 3.4 collective-permute-start.2
  260.1 3.8 collective-permute-done.2
  268.1 2.4 collective-permute-start.1
  270.6 2.0 fusion.155
  284.5 3.0 conditional.23
  295.0 2.2 collective-permute-start.2
  297.6 5.3 %collective-permute-done.3 = f32[512,128]{1,0:T(8,128)} collective-permute-done((f32[512,128]{1,0:T(8,128)S(1)}, f32[512,128]{1,0:T(8,128)}, u32[]{:S(2)}, u32[]{:S(2)}) %collective-permute-start.3) | collective-permute-done | bytes 262176 | tf_op jit(solution)/shard_map/while/body/eval_jaxpr/ppermute | solution.py:12
  303.0 2.8 collective-permute-done.2
  310.3 2.0 fusion.155
  324.3 3.0 conditional.23
  336.9 5.6 %collective-permute-done.3 = f32[512,128]{1,0:T(8,128)} collective-permute-done((f32[512,128]{1,0:T(8,128)S(1)}, f32[512,128]{1,0:T(8,128)}, u32[]{:S(2)}, u32[]{:S(2)}) %collective-permute-start.3) | collective-permute-done | bytes 262176 | tf_op jit(solution)/shard_map/while/body/eval_jaxpr/ppermute | solution.py:12
  342.5 2.8 collective-permute-done.2
  350.2 2.0 fusion.155
  364.2 3.0 conditional.23
  374.3 2.1 collective-permute-start.2
  376.9 5.0 %collective-permute-done.3 = f32[512,128]{1,0:T(8,128)} collective-permute-done((f32[512,128]{1,0:T(8,128)S(1)}, f32[512,128]{1,0:T(8,128)}, u32[]{:S(2)}, u32[]{:S(2)}) %collective-permute-start.3) | collective-permute-done | bytes 262176 | tf_op jit(solution)/shard_map/while/body/eval_jaxpr/ppermute | solution.py:12
  382.0 2.8 collective-permute-done.2
  404.3 3.0 conditional.23
  416.5 4.5 collective-permute-done.3
  421.0 3.2 collective-permute-done.2
  428.2 2.5 conditional.10
  431.6 3.5 conditional.8
  442.2 8.4 %collective-permute-done.4 = f32[512,128]{1,0:T(8,128)S(1)} collective-permute-done((f32[512,128]{1,0:T(8,128)S(1)}, f32[512,128]{1,0:T(8,128)S(1)}, u32[]{:S(2)}, u32[]{:S(2)}) %collective-permute-start.4) | collective-permute-done | bytes 262176 | tf_op jit(solution)/shard_map/ppermute | solution.py:12
  455.0 3.5 all-to-all-start.4
  458.6 3.0 collective-permute-done.5
  461.6 5.7 %all-to-all-done.4 = bf16[4,512,128]{2,0,1:T(4,128)(2,1)S(1)} async-done(((bf16[4,512,128]{2,0,1:T(4,128)(2,1)}), bf16[4,512,128]{2,0,1:T(4,128)(2,1)S(1)}, u32[]{:S(2)}, u32[]{:S(2)}) %all-to-all-start.4) | async-done | bytes 524320 | tf_op jit(solution)/shard_map/all_to_all | solution.py:138
  471.3 21.4 %reduce-scatter.5.cloned.1.call-done = f32[128,128]{1,0:T(8,128)} async-done(((f32[512,128]{1,0:T(8,128)}), f32[128,128]{1,0:T(8,128)}) %reduce-scatter.5.cloned.1.call-update) | async-done | bytes 65552 | tf_op jit(solution)/shard_map/reduce_scatter | solution.py:133
  (658 shorter events, 213.9 us)
Async XLA Ops:
  27.5 77.8 %all-to-all-start.2 = ((bf16[16,128,128]{2,1,0:T(8,128)(2,1)}), bf16[16,128,128]{2,1,0:T(8,128)(2,1)S(1)}, u32[]{:S(2)}, u32[]{:S(2)}) async-start(bf16[16,128,128]{2,1,0:T(8,128)(2,1)} %param.29), calls=%async_computation.2 | async-start | bytes 1048576 | tf_op jit(solution)/shard_map/all_to_all | solution.py:45
  105.3 3.7 copy-start.48
  105.3 28.4 %all-to-all-start.3 = ((bf16[16,128,128]{2,1,0:T(8,128)(2,1)}), bf16[16,128,128]{2,1,0:T(8,128)(2,1)S(1)}, u32[]{:S(2)}, u32[]{:S(2)}) async-start(bf16[16,128,128]{2,1,0:T(8,128)(2,1)} %param.28), calls=%async_computation.3 | async-start | bytes 1048576 | tf_op jit(solution)/shard_map/all_to_all | solution.py:44
  108.9 361.0 %reduce-scatter.3.cloned.1.call-start = ((), (), s32[]{:S(2)}) async-start(), calls=%async_computation.7 | async-start | bytes 327680 | tf_op jit(solution)/shard_map/reduce_scatter | solution.py:132
  119.7 5.1 %copy-start.49 = (bf16[128,128]{1,0:T(8,128)(2,1)S(1)}, bf16[128,128]{1,0:T(8,128)(2,1)}, u32[]{:S(2)}) copy-start(bf16[128,128]{1,0:T(8,128)(2,1)} %param.27) | copy-start | bytes 98308
  139.7 11.5 %copy-start.44 = (s32[512]{0:T(512)}, s32[512]{0:T(512)S(1)}, u32[]{:S(2)}) copy-start(s32[512]{0:T(512)S(1)} %get-tuple-element.931) | copy-start | bytes 6148 | tf_op jit(solution)/shard_map/while
  141.3 28.8 %collective-permute-start = (bf16[512,128]{1,0:T(8,128)(2,1)}, bf16[512,128]{1,0:T(8,128)(2,1)}, u32[]{:S(2)}, u32[]{:S(2)}) collective-permute-start(bf16[512,128]{1,0:T(8,128)(2,1)} %copy.129), channel_id=1, source_target_pairs={{7,0},{0,1},{1,2},{2,3},{3,4},{4,5},{5,6},{6,7},{15,8},{8,9},{9,10... | collective-permute-start | bytes 393224 | tf_op jit(solution)/shard_map/while/body/eval_jaxpr/ppermute | solution.py:12
  142.8 27.2 %collective-permute-start.1 = (bf16[512,128]{1,0:T(8,128)(2,1)}, bf16[512,128]{1,0:T(8,128)(2,1)}, u32[]{:S(2)}, u32[]{:S(2)}) collective-permute-start(bf16[512,128]{1,0:T(8,128)(2,1)} %copy.130), channel_id=1, source_target_pairs={{7,0},{0,1},{1,2},{2,3},{3,4},{4,5},{5,6},{6,7},{15,8},{8,9},{9,10... | collective-permute-start | bytes 393224 | tf_op jit(solution)/shard_map/while/body/eval_jaxpr/ppermute | solution.py:12
  151.9 2.6 copy-start.38
  166.4 12.0 %collective-permute-start.3 = (f32[512,128]{1,0:T(8,128)S(1)}, f32[512,128]{1,0:T(8,128)}, u32[]{:S(2)}, u32[]{:S(2)}) collective-permute-start(f32[512,128]{1,0:T(8,128)S(1)} %maximum_add_fusion.10), channel_id=1, source_target_pairs={{7,0},{0,1},{1,2},{2,3},{3,4},{4,5},{5,6},{6,7},{15,8},{8,9},{9,10... | collective-permute-start | bytes 786440 | tf_op jit(solution)/shard_map/while/body/eval_jaxpr/ppermute | solution.py:12
  169.1 13.8 %collective-permute-start.2 = (f32[512,128]{1,0:T(8,128)}, f32[512,128]{1,0:T(8,128)}, u32[]{:S(2)}, u32[]{:S(2)}) collective-permute-start(f32[512,128]{1,0:T(8,128)} %maximum_add_fusion.9), channel_id=1, source_target_pairs={{7,0},{0,1},{1,2},{2,3},{3,4},{4,5},{5,6},{6,7},{15,8},{8,9},{9,10... | collective-permute-start | bytes 786440 | tf_op jit(solution)/shard_map/while/body/eval_jaxpr/ppermute | solution.py:12
  183.7 11.0 %copy-start.44 = (s32[512]{0:T(512)}, s32[512]{0:T(512)S(1)}, u32[]{:S(2)}) copy-start(s32[512]{0:T(512)S(1)} %get-tuple-element.931) | copy-start | bytes 6148 | tf_op jit(solution)/shard_map/while
  185.2 28.1 %collective-permute-start = (bf16[512,128]{1,0:T(8,128)(2,1)}, bf16[512,128]{1,0:T(8,128)(2,1)}, u32[]{:S(2)}, u32[]{:S(2)}) collective-permute-start(bf16[512,128]{1,0:T(8,128)(2,1)} %copy.129), channel_id=1, source_target_pairs={{7,0},{0,1},{1,2},{2,3},{3,4},{4,5},{5,6},{6,7},{15,8},{8,9},{9,10... | collective-permute-start | bytes 393224 | tf_op jit(solution)/shard_map/while/body/eval_jaxpr/ppermute | solution.py:12
  186.8 26.5 %collective-permute-start.1 = (bf16[512,128]{1,0:T(8,128)(2,1)}, bf16[512,128]{1,0:T(8,128)(2,1)}, u32[]{:S(2)}, u32[]{:S(2)}) collective-permute-start(bf16[512,128]{1,0:T(8,128)(2,1)} %copy.130), channel_id=1, source_target_pairs={{7,0},{0,1},{1,2},{2,3},{3,4},{4,5},{5,6},{6,7},{15,8},{8,9},{9,10... | collective-permute-start | bytes 393224 | tf_op jit(solution)/shard_map/while/body/eval_jaxpr/ppermute | solution.py:12
  208.2 12.1 %collective-permute-start.3 = (f32[512,128]{1,0:T(8,128)S(1)}, f32[512,128]{1,0:T(8,128)}, u32[]{:S(2)}, u32[]{:S(2)}) collective-permute-start(f32[512,128]{1,0:T(8,128)S(1)} %maximum_add_fusion.10), channel_id=1, source_target_pairs={{7,0},{0,1},{1,2},{2,3},{3,4},{4,5},{5,6},{6,7},{15,8},{8,9},{9,10... | collective-permute-start | bytes 786440 | tf_op jit(solution)/shard_map/while/body/eval_jaxpr/ppermute | solution.py:12
  210.9 13.0 %collective-permute-start.2 = (f32[512,128]{1,0:T(8,128)}, f32[512,128]{1,0:T(8,128)}, u32[]{:S(2)}, u32[]{:S(2)}) collective-permute-start(f32[512,128]{1,0:T(8,128)} %maximum_add_fusion.9), channel_id=1, source_target_pairs={{7,0},{0,1},{1,2},{2,3},{3,4},{4,5},{5,6},{6,7},{15,8},{8,9},{9,10... | collective-permute-start | bytes 786440 | tf_op jit(solution)/shard_map/while/body/eval_jaxpr/ppermute | solution.py:12
  224.5 11.0 %copy-start.44 = (s32[512]{0:T(512)}, s32[512]{0:T(512)S(1)}, u32[]{:S(2)}) copy-start(s32[512]{0:T(512)S(1)} %get-tuple-element.931) | copy-start | bytes 6148 | tf_op jit(solution)/shard_map/while
  226.1 32.0 %collective-permute-start = (bf16[512,128]{1,0:T(8,128)(2,1)}, bf16[512,128]{1,0:T(8,128)(2,1)}, u32[]{:S(2)}, u32[]{:S(2)}) collective-permute-start(bf16[512,128]{1,0:T(8,128)(2,1)} %copy.129), channel_id=1, source_target_pairs={{7,0},{0,1},{1,2},{2,3},{3,4},{4,5},{5,6},{6,7},{15,8},{8,9},{9,10... | collective-permute-start | bytes 393224 | tf_op jit(solution)/shard_map/while/body/eval_jaxpr/ppermute | solution.py:12
  227.6 30.5 %collective-permute-start.1 = (bf16[512,128]{1,0:T(8,128)(2,1)}, bf16[512,128]{1,0:T(8,128)(2,1)}, u32[]{:S(2)}, u32[]{:S(2)}) collective-permute-start(bf16[512,128]{1,0:T(8,128)(2,1)} %copy.130), channel_id=1, source_target_pairs={{7,0},{0,1},{1,2},{2,3},{3,4},{4,5},{5,6},{6,7},{15,8},{8,9},{9,10... | collective-permute-start | bytes 393224 | tf_op jit(solution)/shard_map/while/body/eval_jaxpr/ppermute | solution.py:12
  248.0 3.7 copy-start.1
  248.0 3.7 copy-start.3
  249.0 11.0 %collective-permute-start.3 = (f32[512,128]{1,0:T(8,128)S(1)}, f32[512,128]{1,0:T(8,128)}, u32[]{:S(2)}, u32[]{:S(2)}) collective-permute-start(f32[512,128]{1,0:T(8,128)S(1)} %maximum_add_fusion.10), channel_id=1, source_target_pairs={{7,0},{0,1},{1,2},{2,3},{3,4},{4,5},{5,6},{6,7},{15,8},{8,9},{9,10... | collective-permute-start | bytes 786440 | tf_op jit(solution)/shard_map/while/body/eval_jaxpr/ppermute | solution.py:12
  254.3 9.6 %collective-permute-start.2 = (f32[512,128]{1,0:T(8,128)}, f32[512,128]{1,0:T(8,128)}, u32[]{:S(2)}, u32[]{:S(2)}) collective-permute-start(f32[512,128]{1,0:T(8,128)} %maximum_add_fusion.9), channel_id=1, source_target_pairs={{7,0},{0,1},{1,2},{2,3},{3,4},{4,5},{5,6},{6,7},{15,8},{8,9},{9,10... | collective-permute-start | bytes 786440 | tf_op jit(solution)/shard_map/while/body/eval_jaxpr/ppermute | solution.py:12
  264.5 13.9 %copy-start.44 = (s32[512]{0:T(512)}, s32[512]{0:T(512)S(1)}, u32[]{:S(2)}) copy-start(s32[512]{0:T(512)S(1)} %get-tuple-element.931) | copy-start | bytes 6148 | tf_op jit(solution)/shard_map/while
  266.1 31.5 %collective-permute-start = (bf16[512,128]{1,0:T(8,128)(2,1)}, bf16[512,128]{1,0:T(8,128)(2,1)}, u32[]{:S(2)}, u32[]{:S(2)}) collective-permute-start(bf16[512,128]{1,0:T(8,128)(2,1)} %copy.129), channel_id=1, source_target_pairs={{7,0},{0,1},{1,2},{2,3},{3,4},{4,5},{5,6},{6,7},{15,8},{8,9},{9,10... | collective-permute-start | bytes 393224 | tf_op jit(solution)/shard_map/while/body/eval_jaxpr/ppermute | solution.py:12
  268.1 29.5 %collective-permute-start.1 = (bf16[512,128]{1,0:T(8,128)(2,1)}, bf16[512,128]{1,0:T(8,128)(2,1)}, u32[]{:S(2)}, u32[]{:S(2)}) collective-permute-start(bf16[512,128]{1,0:T(8,128)(2,1)} %copy.130), channel_id=1, source_target_pairs={{7,0},{0,1},{1,2},{2,3},{3,4},{4,5},{5,6},{6,7},{15,8},{8,9},{9,10... | collective-permute-start | bytes 393224 | tf_op jit(solution)/shard_map/while/body/eval_jaxpr/ppermute | solution.py:12
  291.9 11.0 %collective-permute-start.3 = (f32[512,128]{1,0:T(8,128)S(1)}, f32[512,128]{1,0:T(8,128)}, u32[]{:S(2)}, u32[]{:S(2)}) collective-permute-start(f32[512,128]{1,0:T(8,128)S(1)} %maximum_add_fusion.10), channel_id=1, source_target_pairs={{7,0},{0,1},{1,2},{2,3},{3,4},{4,5},{5,6},{6,7},{15,8},{8,9},{9,10... | collective-permute-start | bytes 786440 | tf_op jit(solution)/shard_map/while/body/eval_jaxpr/ppermute | solution.py:12
  295.0 10.8 %collective-permute-start.2 = (f32[512,128]{1,0:T(8,128)}, f32[512,128]{1,0:T(8,128)}, u32[]{:S(2)}, u32[]{:S(2)}) collective-permute-start(f32[512,128]{1,0:T(8,128)} %maximum_add_fusion.9), channel_id=1, source_target_pairs={{7,0},{0,1},{1,2},{2,3},{3,4},{4,5},{5,6},{6,7},{15,8},{8,9},{9,10... | collective-permute-start | bytes 786440 | tf_op jit(solution)/shard_map/while/body/eval_jaxpr/ppermute | solution.py:12
  306.4 11.8 %copy-start.44 = (s32[512]{0:T(512)}, s32[512]{0:T(512)S(1)}, u32[]{:S(2)}) copy-start(s32[512]{0:T(512)S(1)} %get-tuple-element.931) | copy-start | bytes 6148 | tf_op jit(solution)/shard_map/while
  308.0 28.9 %collective-permute-start = (bf16[512,128]{1,0:T(8,128)(2,1)}, bf16[512,128]{1,0:T(8,128)(2,1)}, u32[]{:S(2)}, u32[]{:S(2)}) collective-permute-start(bf16[512,128]{1,0:T(8,128)(2,1)} %copy.129), channel_id=1, source_target_pairs={{7,0},{0,1},{1,2},{2,3},{3,4},{4,5},{5,6},{6,7},{15,8},{8,9},{9,10... | collective-permute-start | bytes 393224 | tf_op jit(solution)/shard_map/while/body/eval_jaxpr/ppermute | solution.py:12
  309.6 27.3 %collective-permute-start.1 = (bf16[512,128]{1,0:T(8,128)(2,1)}, bf16[512,128]{1,0:T(8,128)(2,1)}, u32[]{:S(2)}, u32[]{:S(2)}) collective-permute-start(bf16[512,128]{1,0:T(8,128)(2,1)} %copy.130), channel_id=1, source_target_pairs={{7,0},{0,1},{1,2},{2,3},{3,4},{4,5},{5,6},{6,7},{15,8},{8,9},{9,10... | collective-permute-start | bytes 393224 | tf_op jit(solution)/shard_map/while/body/eval_jaxpr/ppermute | solution.py:12
  331.7 10.8 %collective-permute-start.3 = (f32[512,128]{1,0:T(8,128)S(1)}, f32[512,128]{1,0:T(8,128)}, u32[]{:S(2)}, u32[]{:S(2)}) collective-permute-start(f32[512,128]{1,0:T(8,128)S(1)} %maximum_add_fusion.10), channel_id=1, source_target_pairs={{7,0},{0,1},{1,2},{2,3},{3,4},{4,5},{5,6},{6,7},{15,8},{8,9},{9,10... | collective-permute-start | bytes 786440 | tf_op jit(solution)/shard_map/while/body/eval_jaxpr/ppermute | solution.py:12
  334.8 10.5 %collective-permute-start.2 = (f32[512,128]{1,0:T(8,128)}, f32[512,128]{1,0:T(8,128)}, u32[]{:S(2)}, u32[]{:S(2)}) collective-permute-start(f32[512,128]{1,0:T(8,128)} %maximum_add_fusion.9), channel_id=1, source_target_pairs={{7,0},{0,1},{1,2},{2,3},{3,4},{4,5},{5,6},{6,7},{15,8},{8,9},{9,10... | collective-permute-start | bytes 786440 | tf_op jit(solution)/shard_map/while/body/eval_jaxpr/ppermute | solution.py:12
  346.0 12.2 %copy-start.44 = (s32[512]{0:T(512)}, s32[512]{0:T(512)S(1)}, u32[]{:S(2)}) copy-start(s32[512]{0:T(512)S(1)} %get-tuple-element.931) | copy-start | bytes 6148 | tf_op jit(solution)/shard_map/while
  347.5 29.4 %collective-permute-start = (bf16[512,128]{1,0:T(8,128)(2,1)}, bf16[512,128]{1,0:T(8,128)(2,1)}, u32[]{:S(2)}, u32[]{:S(2)}) collective-permute-start(bf16[512,128]{1,0:T(8,128)(2,1)} %copy.129), channel_id=1, source_target_pairs={{7,0},{0,1},{1,2},{2,3},{3,4},{4,5},{5,6},{6,7},{15,8},{8,9},{9,10... | collective-permute-start | bytes 393224 | tf_op jit(solution)/shard_map/while/body/eval_jaxpr/ppermute | solution.py:12
  349.1 27.8 %collective-permute-start.1 = (bf16[512,128]{1,0:T(8,128)(2,1)}, bf16[512,128]{1,0:T(8,128)(2,1)}, u32[]{:S(2)}, u32[]{:S(2)}) collective-permute-start(bf16[512,128]{1,0:T(8,128)(2,1)} %copy.130), channel_id=1, source_target_pairs={{7,0},{0,1},{1,2},{2,3},{3,4},{4,5},{5,6},{6,7},{15,8},{8,9},{9,10... | collective-permute-start | bytes 393224 | tf_op jit(solution)/shard_map/while/body/eval_jaxpr/ppermute | solution.py:12
  371.6 10.3 %collective-permute-start.3 = (f32[512,128]{1,0:T(8,128)S(1)}, f32[512,128]{1,0:T(8,128)}, u32[]{:S(2)}, u32[]{:S(2)}) collective-permute-start(f32[512,128]{1,0:T(8,128)S(1)} %maximum_add_fusion.10), channel_id=1, source_target_pairs={{7,0},{0,1},{1,2},{2,3},{3,4},{4,5},{5,6},{6,7},{15,8},{8,9},{9,10... | collective-permute-start | bytes 786440 | tf_op jit(solution)/shard_map/while/body/eval_jaxpr/ppermute | solution.py:12
  374.3 10.4 %collective-permute-start.2 = (f32[512,128]{1,0:T(8,128)}, f32[512,128]{1,0:T(8,128)}, u32[]{:S(2)}, u32[]{:S(2)}) collective-permute-start(f32[512,128]{1,0:T(8,128)} %maximum_add_fusion.9), channel_id=1, source_target_pairs={{7,0},{0,1},{1,2},{2,3},{3,4},{4,5},{5,6},{6,7},{15,8},{8,9},{9,10... | collective-permute-start | bytes 786440 | tf_op jit(solution)/shard_map/while/body/eval_jaxpr/ppermute | solution.py:12
  385.5 12.8 %copy-start.44 = (s32[512]{0:T(512)}, s32[512]{0:T(512)S(1)}, u32[]{:S(2)}) copy-start(s32[512]{0:T(512)S(1)} %get-tuple-element.931) | copy-start | bytes 6148 | tf_op jit(solution)/shard_map/while
  387.0 29.5 %collective-permute-start = (bf16[512,128]{1,0:T(8,128)(2,1)}, bf16[512,128]{1,0:T(8,128)(2,1)}, u32[]{:S(2)}, u32[]{:S(2)}) collective-permute-start(bf16[512,128]{1,0:T(8,128)(2,1)} %copy.129), channel_id=1, source_target_pairs={{7,0},{0,1},{1,2},{2,3},{3,4},{4,5},{5,6},{6,7},{15,8},{8,9},{9,10... | collective-permute-start | bytes 393224 | tf_op jit(solution)/shard_map/while/body/eval_jaxpr/ppermute | solution.py:12
  388.6 27.9 %collective-permute-start.1 = (bf16[512,128]{1,0:T(8,128)(2,1)}, bf16[512,128]{1,0:T(8,128)(2,1)}, u32[]{:S(2)}, u32[]{:S(2)}) collective-permute-start(bf16[512,128]{1,0:T(8,128)(2,1)} %copy.130), channel_id=1, source_target_pairs={{7,0},{0,1},{1,2},{2,3},{3,4},{4,5},{5,6},{6,7},{15,8},{8,9},{9,10... | collective-permute-start | bytes 393224 | tf_op jit(solution)/shard_map/while/body/eval_jaxpr/ppermute | solution.py:12
  398.9 2.6 copy-start.38
  411.7 9.2 %collective-permute-start.3 = (f32[512,128]{1,0:T(8,128)S(1)}, f32[512,128]{1,0:T(8,128)}, u32[]{:S(2)}, u32[]{:S(2)}) collective-permute-start(f32[512,128]{1,0:T(8,128)S(1)} %maximum_add_fusion.10), channel_id=1, source_target_pairs={{7,0},{0,1},{1,2},{2,3},{3,4},{4,5},{5,6},{6,7},{15,8},{8,9},{9,10... | collective-permute-start | bytes 786440 | tf_op jit(solution)/shard_map/while/body/eval_jaxpr/ppermute | solution.py:12
  414.8 9.4 %collective-permute-start.2 = (f32[512,128]{1,0:T(8,128)}, f32[512,128]{1,0:T(8,128)}, u32[]{:S(2)}, u32[]{:S(2)}) collective-permute-start(f32[512,128]{1,0:T(8,128)} %maximum_add_fusion.9), channel_id=1, source_target_pairs={{7,0},{0,1},{1,2},{2,3},{3,4},{4,5},{5,6},{6,7},{15,8},{8,9},{9,10... | collective-permute-start | bytes 786440 | tf_op jit(solution)/shard_map/while/body/eval_jaxpr/ppermute | solution.py:12
  440.7 9.9 %collective-permute-start.4 = (f32[512,128]{1,0:T(8,128)S(1)}, f32[512,128]{1,0:T(8,128)S(1)}, u32[]{:S(2)}, u32[]{:S(2)}) collective-permute-start(f32[512,128]{1,0:T(8,128)S(1)} %maximum_add_fusion.4), channel_id=1, source_target_pairs={{7,0},{0,1},{1,2},{2,3},{3,4},{4,5},{5,6},{6,7},{15,8},{8,9},{9,10... | collective-permute-start | bytes 786440 | tf_op jit(solution)/shard_map/ppermute | solution.py:12
  452.3 9.2 %collective-permute-start.5 = (f32[512,128]{1,0:T(8,128)S(1)}, f32[512,128]{1,0:T(8,128)}, u32[]{:S(2)}, u32[]{:S(2)}) collective-permute-start(f32[512,128]{1,0:T(8,128)S(1)} %maximum_add_fusion.5), channel_id=1, source_target_pairs={{7,0},{0,1},{1,2},{2,3},{3,4},{4,5},{5,6},{6,7},{15,8},{8,9},{9,10... | collective-permute-start | bytes 786440 | tf_op jit(solution)/shard_map/ppermute | solution.py:12
  455.0 12.3 %all-to-all-start.4 = ((bf16[4,512,128]{2,0,1:T(4,128)(2,1)}), bf16[4,512,128]{2,0,1:T(4,128)(2,1)S(1)}, u32[]{:S(2)}, u32[]{:S(2)}) async-start(bf16[4,512,128]{2,0,1:T(4,128)(2,1)} %copy.75), calls=%async_computation.4 | async-start | bytes 1048576 | tf_op jit(solution)/shard_map/all_to_all | solution.py:138
  458.5 34.2 %reduce-scatter.5.cloned.1.call-start = ((), (), s32[]{:S(2)}) async-start(), calls=%async_computation.8 | async-start | bytes 327680 | tf_op jit(solution)/shard_map/reduce_scatter | solution.py:133
  (142 other events, 138.7 us)
Sparse Core Ops, SparseCore 0:
  451.5 18.3 reduce-scatter.2
  472.5 20.1 reduce-scatter.4
where the time goes:
time: 506 us; the launch traced here: 501 us
  local copies, waits for them, and re-layouts  118 us (23%)
  blocking collectives  108 us (21%)
  waiting for transfers between devices  102 us (20%)
  other arithmetic  53 us (10%)
  loops' own time  37.2 us (7%)
  starting transfers between devices  35.4 us (7%)
  matrix products  28.2 us (6%)
  between operations  19.5 us (4%)
    ppermute x30, waiting for transfers between devices, from_behind(): return lax.ppermute(block, axis, route)  72.9 us
    all_gather x1, blocking collectives, local(): all_places = lax.all_gather(positions, ('head', 'ctx'), axis=0, tiled=True)  71.4 us
    while x224, local copies, waits for them, and re-layouts  57.2 us
    another operation x1, loops' own time, local(): lax.fori_loop(0, rounds, advance, (key_block, value_block, zero_rows, zer...  36.2 us
    ppermute x30, starting transfers between devices, from_behind(): return lax.ppermute(block, axis, route)  24.8 us
    reduce_scatter x1, waiting for transfers between devices, local(): lax.psum_scatter(value_sums, 'head', scatter_dimension=0, tiled=True)  21.4 us
    reduce_min x8, other arithmetic, block_terms(): visible = jnp.max(query_at) >= jnp.min(key_at)  16.1 us
    all_to_all x1, blocking collectives, local(): lax.all_to_all(queries, 'head', split_axis=0, concat_axis=1, tiled=True)  12.3 us
  transfers between devices with their start and end apart: 35, of which 19 were waited for; matrix products, arithmetic and copies ran while one was open for 23% of the time, Pallas kernels for 0%

commit v1 on v0

v1 whole, which is shorter than its diff:
```python
import functools
import math

import jax
import jax.numpy as jnp
from jax import lax
from jax.experimental import pallas as pl
from jax.experimental.pallas import tpu as pltpu
from jax.sharding import PartitionSpec as P


def contract(a, b, axes):
    return lax.dot_general(a, b, (axes, ((), ())), preferred_element_type=jnp.float32)


def tiles_kernel(cycle, runs_ref, mine_ref, qd_ref, lse_ref, delta_ref, kv_ref, dq_ref, dkv_ref, acc):
    heads, rows, wide = qd_ref.shape
    width = wide // 2
    run = rows // 2
    scaling = width ** (-0.5)
    log2e = 1.0 / math.log(2.0)
    me = mine_ref[0]
    my_run = runs_ref[me]
    acc[...] = jnp.zeros_like(acc)

    def unit(query_half, key_row, diagonal):
        rows_of = pl.ds(pl.multiple_of(query_half * run, run), run)
        keys_of = pl.ds(pl.multiple_of(key_row, run), run)
        query = qd_ref[:, rows_of, :width].reshape(heads * run, width)
        grad = qd_ref[:, rows_of, width:].reshape(heads * run, width)
        key = kv_ref[keys_of, :width]
        value = kv_ref[keys_of, width:]
        scores = contract(key, query, ((1,), (1,)))
        prob = jnp.exp2(scores * (scaling * log2e) - lse_ref[query_half] * log2e)
        if diagonal:
            key_at = lax.broadcasted_iota(jnp.int32, scores.shape, 0)
            query_at = lax.broadcasted_iota(jnp.int32, scores.shape, 1) % run
            prob = jnp.where(key_at <= query_at, prob, 0.0)
        grad_prob = contract(value, grad, ((1,), (1,)))
        grad_score = (prob * (grad_prob - delta_ref[query_half])).astype(jnp.bfloat16)
        value_grad = contract(prob.astype(jnp.bfloat16), grad, ((1,), (0,)))
        key_grad = contract(grad_score, query, ((1,), (0,)))
        acc[query_half] += contract(key.T, grad_score, ((1,), (0,)))
        return keys_of, key_grad * scaling, value_grad

    def put(terms):
        keys_of, key_grad, value_grad = terms
        dkv_ref[keys_of, :width] = key_grad
        dkv_ref[keys_of, width:] = value_grad

    def add(terms):
        keys_of, key_grad, value_grad = terms
        dkv_ref[keys_of, :width] += key_grad
        dkv_ref[keys_of, width:] += value_grad

    put(unit(1, me * rows, False))
    add(unit(0, me * rows, True))
    put(unit(1, me * rows + run, True))

    @pl.loop(1, cycle)
    def _(step):
        other = lax.rem(me + step, cycle)
        first = other * rows
        late = (runs_ref[other] > my_run).astype(jnp.int32)
        put(unit(1, first, False))
        dkv_ref[pl.ds(pl.multiple_of(first + run, run), run), :] = jnp.zeros((run, wide), jnp.float32)
        add(unit(late, first + late * run, False))

    for half in range(2):
        for head in range(heads):
            part = acc[half, :, head * run : (head + 1) * run] * scaling
            dq_ref[head, half * run : (half + 1) * run, :] = part.T.astype(jnp.bfloat16)


def tiles(cycle, runs, mine, qd, lse, delta, kv):
    heads, rows, wide = qd.shape
    whole = pl.BlockSpec(memory_space=pltpu.VMEM)
    scalars = pl.BlockSpec(memory_space=pltpu.SMEM)
    return pl.pallas_call(
        functools.partial(tiles_kernel, cycle),
        out_shape=(
            jax.ShapeDtypeStruct((heads, rows, wide // 2), jnp.bfloat16),
            jax.ShapeDtypeStruct(kv.shape, jnp.float32),
        ),
        in_specs=[scalars, scalars, whole, whole, whole, whole],
        out_specs=(whole, whole),
        scratch_shapes=[pltpu.VMEM((2, wide // 2, heads * rows // 2), jnp.float32)],
        compiler_params=pltpu.CompilerParams(vmem_limit_bytes=60 * 1024 * 1024),
    )(runs, mine, qd, lse, delta, kv)


def local(queries, key_rows, value_rows, attn_output, grad_output, logsumexp, positions):
    cycle = lax.axis_size("ctx")
    group = lax.axis_size("head")
    width = queries.shape[2]
    rows = positions.shape[0] * group
    run = rows // 2
    heads = queries.shape[0] // group
    row_delta = jnp.sum(grad_output.astype(jnp.float32) * attn_output.astype(jnp.float32), axis=2)
    kv = lax.all_gather(
        jnp.concatenate([key_rows, value_rows], axis=1), ("ctx", "head"), axis=0, tiled=True
    )
    places = lax.all_gather(positions, ("ctx", "head"), axis=0, tiled=True)
    runs = places.reshape(cycle, rows)[:, 0] // run
    mine = lax.axis_index("ctx").reshape(1)
    qd = lax.all_to_all(
        jnp.concatenate([queries, grad_output], axis=2), "head", split_axis=0, concat_axis=1, tiled=True
    )
    stats = lax.all_to_all(
        jnp.stack([logsumexp, row_delta], axis=1), "head", split_axis=0, concat_axis=2, tiled=True
    )
    stats = stats.reshape(heads, 2, 2, run).transpose(1, 2, 0, 3).reshape(2, 2, 1, heads * run)
    dq, dkv = tiles(cycle, runs, mine, qd, stats[0], stats[1], kv)
    mine_kv = lax.psum_scatter(dkv, ("ctx", "head"), scatter_dimension=0, tiled=True)
    grad_queries = lax.all_to_all(dq, "head", split_axis=1, concat_axis=0, tiled=True)
    return (
        grad_queries,
        mine_kv[:, :width].astype(jnp.bfloat16),
        mine_kv[:, width:].astype(jnp.bfloat16),
    )


def solution(mesh):
    return jax.shard_map(
        local,
        mesh=mesh,
        in_specs=(
            P(None, ("ctx", "head"), None),
            P(("ctx", "head"), None),
            P(("ctx", "head"), None),
            P(None, ("ctx", "head"), None),
            P(None, ("ctx", "head"), None),
            P(None, ("ctx", "head")),
            P(("ctx", "head")),
        ),
        out_specs=(
            P(None, ("ctx", "head"), None),
            P(("ctx", "head"), None),
            P(("ctx", "head"), None),
        ),
        check_vma=False,
    )
```

time: 506 us -> 238 us (0.47)
  local copies, waits for them, and re-layouts: 118 us -> 5.9 us
  blocking collectives: 108 us -> 62 us
  other arithmetic: 53 us -> 8.78 us
  loops' own time: 37.2 us -> 0 us
  matrix products: 28.2 us -> 0 us
  starting transfers between devices: 35.4 us -> 7.81 us
  waiting for transfers between devices: 102 us -> 122 us
  Pallas kernels: 0 us -> 16.4 us
  between operations: 19.5 us -> 14.1 us
    reduce_scatter x2 -> x1, waiting for transfers between devices: 23.1 us -> 120 us  [local(): lax.psum_scatter(dkv, ('ctx', 'head'), scatter_dimension=0, tiled=True)]
    ppermute x30 -> x0, waiting for transfers between devices: 72.9 us -> none  [from_behind(): return lax.ppermute(block, axis, route)]
    while x224 -> x0, local copies, waits for them, and re-layouts: 57.2 us -> none
    all_gather x3 -> x1, blocking collectives: 88.1 us -> 47.7 us  [local(): places = lax.all_gather(positions, ('ctx', 'head'), axis=0, tiled=True)]
    another operation x33 -> x0, loops' own time: 37.2 us -> none  [the longest x1 36.2 us: local(): lax.fori_loop(0, rounds, advance, (key_block, value_block, zero_rows, zer...]
    slice x32 -> x5, local copies, waits for them, and re-layouts: 34.5 us -> 0.64 us  [the longest x1 0.63 us: local(): mine_kv[:, width:].astype(jnp.bfloat16)]
    add x71 -> x0, other arithmetic: 31.7 us -> none  [the longest x7 11.8 us: advance(): key_acc + key_grad]
    dot_general x85 -> x0, matrix products: 28.2 us -> none  [the longest x17 6.51 us: tile_terms(): jnp.einsum('hqd,kd->hqk', query_run, key_run, preferred_element_type=jnp....]
  transfers between devices with their start and end apart: 35 -> 4, of which waited for: 19 -> 2; matrix products, arithmetic and copies ran while one was open for 23% -> 5% of each run, Pallas kernels for 0% -> 0%
where the time goes in v1:
time: 238 us; the launch traced here: 237 us
  waiting for transfers between devices  122 us (51%)
  blocking collectives  62 us (26%)
  Pallas kernels  16.4 us (7%)
  between operations  14.1 us (6%)
  other arithmetic  8.78 us (4%)
  starting transfers between devices  7.81 us (3%)
  local copies, waits for them, and re-layouts  5.9 us (2%)
    reduce_scatter x1, waiting for transfers between devices, local(): lax.psum_scatter(dkv, ('ctx', 'head'), scatter_dimension=0, tiled=True)  120 us
    all_gather x1, blocking collectives, local(): places = lax.all_gather(positions, ('ctx', 'head'), axis=0, tiled=True)  47.7 us
    pallas_call x1, Pallas kernels, tiles(): pl.pallas_call(functools.partial(tiles_kernel, cycle), out_shape=(jax.Sha...  16.4 us
    all_to_all x1, blocking collectives, local(): lax.all_to_all(dq, 'head', split_axis=1, concat_axis=0, tiled=True)  14.3 us
  transfers between devices with their start and end apart: 4, of which 2 were waited for; matrix products, arithmetic and copies ran while one was open for 5% of the time, Pallas kernels for 0%

profile of v1, /device:TPU:0, one launch (start us, length us, event | category | flops | bytes accessed | tf_op | source)
XLA Modules:
  0.0 236.9 jit_solution(15713341000902767721)
XLA Ops:
  7.2 0.0 all-gather.3.cloned.1.call-start
  7.2 1.4 pad_maximum_fusion.1
  8.6 0.0 all-gather.3.cloned.1.call-update
  8.6 1.5 multiply_reduce_fusion
  10.2 1.3 pad_maximum_fusion.2
  11.5 4.2 %all-to-all-start.1 = ((f32[16,2,128]{2,1,0:T(2,128)}), f32[16,2,128]{2,1,0:T(2,128)S(1)}, u32[]{:S(2)}, u32[]{:S(2)}) async-start(f32[16,2,128]{2,1,0:T(2,128)} %pad_maximum_fusion.2), calls=%async_computation.1 | async-start | bytes 32768 | tf_op jit(solution)/shard_map/all_to_all | solution.py:109
  15.7 0.0 copy-start.1
  15.7 2.3 pad_maximum_fusion
  18.1 1.5 all-to-all-done.1
  19.6 3.5 %all-to-all-start = ((bf16[16,128,256]{2,1,0:T(8,128)(2,1)}), bf16[16,128,256]{2,1,0:T(8,128)(2,1)S(1)}, u32[]{:S(2)}, u32[]{:S(2)}) async-start(bf16[16,128,256]{2,1,0:T(8,128)(2,1)} %pad_maximum_fusion), calls=%async_computation | async-start | bytes 2097152 | tf_op jit(solution)/shard_map/all_to_all | solution.py:106
  23.1 0.0 reduce-scatter.2.cloned.1.call-start
  23.2 0.0 copy-done.1
  23.2 47.7 %all-gather = s32[32,1,128]{2,1,0:T(1,128)S(1)} all-gather(s32[1,1,128]{2,1,0:T(1,128)S(1)} %bitcast.34), channel_id=1, replica_groups=mesh['head'=4,'ctx'=8] {'ctx','head'}, dimensions={0}, use_global_device_ids=true | all-gather | bytes 16896 | tf_op jit(solution)/shard_map/all_gather | solution.py:103
  70.9 0.5 broadcast.16
  71.4 0.7 reduce.3
  72.1 0.1 copy.24
  72.2 0.6 and_select_fusion.runs_ref
  72.8 0.6 squeeze.11.delta_ref
  73.5 0.6 squeeze.10.lse_ref
  74.1 0.0 all-to-all-done
  74.1 1.1 copy.18
  75.2 0.0 all-gather.3.cloned.1.call-done.kv_ref
  75.2 16.4 %shard_map.94 = (bf16[4,512,128]{2,1,0:T(8,128)(2,1)}, f32[4096,256]{1,0:T(8,128)}) custom-call(s32[8]{0:T(128)} %and_select_fusion.runs_ref, s32[1]{0:T(128)} %bitcast.2.mine_ref, bf16[4,512,256]{2,1,0:T(8,128)(2,1)} %bitcast.26, f32[2,1,1024]{2,1,0:T(1,128)} %squeeze.10.lse_ref, f32[2,1,1024]{2,1,0:T(1,128)} %squeeze.11.delta_ref, ...), custom_call_target="tpu_custom_call" | custom-call | tf_op jit(solution)/shard_map/pallas_call | solution.py:79
  91.6 0.0 copy-start
  91.6 0.0 reduce-scatter.2.cloned.1.call-update
  91.6 1.0 copy-done
  92.6 0.4 copy.22
  93.0 14.3 %all_to_all.51 = bf16[4,512,128]{2,0,1:T(4,128)(2,1)S(1)} all-to-all(bf16[4,512,128]{2,0,1:T(4,128)(2,1)S(1)} %copy.22), channel_id=1, replica_groups=mesh['head'=4,'ctx'=8] {'head'}, dimensions={1} | all-to-all | bytes 1048576 | tf_op jit(solution)/shard_map/all_to_all | solution.py:115
  107.3 0.9 copy.23
  108.2 120.4 %reduce-scatter.2.cloned.1.call-done = f32[128,256]{1,0:T(8,128)} async-done(((f32[4096,256]{1,0:T(8,128)}), f32[128,256]{1,0:T(8,128)}) %reduce-scatter.2.cloned.1.call-update) | async-done | bytes 131088 | tf_op jit(solution)/shard_map/reduce_scatter | solution.py:114
  228.5 0.9 convert.4
  229.4 0.6 fusion
  (7 shorter events, 0.0 us)
Async XLA Ops:
  7.2 68.0 %all-gather.3.cloned.1.call-start = ((), (), s32[]{:S(2)}) async-start(), calls=%async_computation.4 | async-start | bytes 2162688 | tf_op jit(solution)/shard_map/all_gather | solution.py:100
  11.5 8.1 %all-to-all-start.1 = ((f32[16,2,128]{2,1,0:T(2,128)}), f32[16,2,128]{2,1,0:T(2,128)S(1)}, u32[]{:S(2)}, u32[]{:S(2)}) async-start(f32[16,2,128]{2,1,0:T(2,128)} %pad_maximum_fusion.2), calls=%async_computation.1 | async-start | bytes 32768 | tf_op jit(solution)/shard_map/all_to_all | solution.py:109
  15.7 7.4 %copy-start.1 = (s32[128]{0:T(128)S(1)}, s32[128]{0:T(128)}, u32[]{:S(2)}) copy-start(s32[128]{0:T(128)} %param.13) | copy-start | bytes 1540
  19.6 54.5 %all-to-all-start = ((bf16[16,128,256]{2,1,0:T(8,128)(2,1)}), bf16[16,128,256]{2,1,0:T(8,128)(2,1)S(1)}, u32[]{:S(2)}, u32[]{:S(2)}) async-start(bf16[16,128,256]{2,1,0:T(8,128)(2,1)} %pad_maximum_fusion), calls=%async_computation | async-start | bytes 2097152 | tf_op jit(solution)/shard_map/all_to_all | solution.py:106
  23.1 205.4 %reduce-scatter.2.cloned.1.call-start = ((), (), s32[]{:S(2)}) async-start(), calls=%async_computation.5 | async-start | bytes 4325376 | tf_op jit(solution)/shard_map/reduce_scatter | solution.py:114
  91.6 1.0 copy-start
Sparse Core Ops, SparseCore 0:
  11.4 59.1 all-gather.2
  91.7 136.7 reduce-scatter.1

commit v2 on v1

--- a/solution.py
+++ b/solution.py
@@ -89,34 +89,392 @@
     )(runs, mine, qd, lse, delta, kv)
 
 
+MESH = pl.DeviceIdType.MESH
+
+
+def digits_of(cycle):
+    return {8: (4, 2), 32: (4, 4, 2)}.get(cycle, (cycle,))
+
+
+def split_index(index, digits):
+    parts = []
+    for size in reversed(digits):
+        parts.append(lax.rem(index, size))
+        index = lax.div(index, size)
+    return parts[::-1]
+
+
+def join_index(parts, digits):
+    index = 0
+    for part, size in zip(parts, digits):
+        index = index * size + part
+    return index
+
+
+def greet(peers):
+    barrier = pltpu.get_barrier_semaphore()
+    for head, ctx in peers:
+        pl.semaphore_signal(barrier, inc=1, device_id=(head, ctx), device_id_type=MESH)
+    pl.semaphore_wait(barrier, len(peers))
+
+
+def gather_kernel(
+    group, cycle, qd_ref, stats_ref, kv_ref, run_ref, qd_out, stats_out, kv_out, run_out,
+    own_sem, kv_send, kv_recv, qd_send, qd_recv, st_send, st_recv, run_send, run_recv,
+    ring_send, ring_recv, core_send, core_recv,
+):
+    digits = digits_of(cycle)
+    head, ctx = lax.axis_index("head"), lax.axis_index("ctx")
+    place = split_index(ctx, digits)
+    half = group // 2
+    each = qd_ref.shape[0] // group
+    core = lax.rem(head, 2)
+    sibling = head + 1 - 2 * core
+    ahead = [lax.rem(head + k, group) for k in range(group)]
+    behind = [lax.rem(head + group - k, group) for k in range(group)]
+    ctx_ahead = [lax.rem(ctx + k, cycle) for k in range(cycle)]
+    ctx_behind = [lax.rem(ctx + cycle - k, cycle) for k in range(cycle)]
+    greet([(h, ctx) for h in ahead[1:]] + [(head, c) for c in ctx_ahead[1:]])
+
+    def remote(src, dst, send, recv, to):
+        return pltpu.make_async_remote_copy(
+            src_ref=src, dst_ref=dst, send_sem=send, recv_sem=recv, device_id=to, device_id_type=MESH
+        )
+
+    started = []
+
+    def start(copy):
+        copy.start()
+        started.append(copy)
+
+    for k in range(1, group):
+        start(remote(kv_ref, kv_out.at[ctx * group + head], kv_send.at[k], kv_recv.at[k], (ahead[k], ctx)))
+    for k in range(1, cycle):
+        start(remote(run_ref, run_out.at[ctx], run_send.at[k], run_recv.at[k], (head, ctx_ahead[k])))
+    for k in range(1, group):
+        rows = pl.ds(ahead[k] * each, each)
+        start(remote(stats_ref.at[rows], stats_out.at[head], st_send.at[k], st_recv.at[k], (ahead[k], ctx)))
+        start(remote(qd_ref.at[rows], qd_out.at[:, head], qd_send.at[k], qd_recv.at[k], (ahead[k], ctx)))
+    mine = pl.ds(head * each, each)
+    local_copies = [
+        pltpu.make_async_copy(kv_ref, kv_out.at[ctx * group + head], own_sem.at[0]),
+        pltpu.make_async_copy(run_ref, run_out.at[ctx], own_sem.at[1]),
+        pltpu.make_async_copy(stats_ref.at[mine], stats_out.at[head], own_sem.at[2]),
+        pltpu.make_async_copy(qd_ref.at[mine], qd_out.at[:, head], own_sem.at[3]),
+    ]
+    for copy in local_copies:
+        copy.start()
+
+    local_copies[0].wait()
+    for k in range(1, group):
+        remote(
+            kv_ref, kv_out.at[ctx * group + behind[k]], kv_send.at[k], kv_recv.at[k], (behind[k], ctx)
+        ).wait_recv()
+
+    def region(label, owner):
+        at = [lax.rem(p + n - o, n) for p, n, o in zip(place, digits, label)]
+        return kv_out.at[pl.ds(join_index(at, digits) * group + owner * half, half)]
+
+    def forward(label, level):
+        block = region(label, core)
+        for axis in range(level, len(digits)):
+            for k in range(1, digits[axis]):
+                to = list(place)
+                to[axis] = lax.rem(place[axis] + k, digits[axis])
+                farther = list(label)
+                farther[axis] = k
+                slot = join_index(farther, digits)
+                start(
+                    remote(
+                        block, block, ring_send.at[slot], ring_recv.at[slot], (head, join_index(to, digits))
+                    )
+                )
+        return block
+
+    none = [0] * len(digits)
+    forward(none, 0)
+    labels = []
+    held = [none]
+    for axis in range(len(digits)):
+        fresh = []
+        for label in held:
+            for k in range(1, digits[axis]):
+                farther = list(label)
+                farther[axis] = k
+                fresh.append((farther, axis))
+        labels += fresh
+        held = held + [label for label, _ in fresh]
+    for label, axis in labels:
+        slot = join_index(label, digits)
+        block = region(label, core)
+        remote(block, block, ring_send.at[slot], ring_recv.at[slot], (head, ctx)).wait_recv()
+        forward(label, axis + 1)
+        start(remote(block, block, core_send.at[slot], core_recv.at[slot], (sibling, ctx)))
+    for label, axis in labels:
+        slot = join_index(label, digits)
+        block = region(label, 1 - core)
+        remote(block, block, core_send.at[slot], core_recv.at[slot], (sibling, ctx)).wait_recv()
+
+    for k in range(1, cycle):
+        remote(
+            run_ref, run_out.at[ctx_behind[k]], run_send.at[k], run_recv.at[k], (head, ctx_behind[k])
+        ).wait_recv()
+    for k in range(1, group):
+        to = (behind[k], ctx)
+        remote(
+            stats_ref.at[mine], stats_out.at[behind[k]], st_send.at[k], st_recv.at[k], to
+        ).wait_recv()
+        remote(
+            qd_ref.at[mine], qd_out.at[:, behind[k]], qd_send.at[k], qd_recv.at[k], to
+        ).wait_recv()
+    for copy in local_copies[1:]:
+        copy.wait()
+    for copy in started:
+        copy.wait_send()
+
+
+def gather(group, cycle, qd, stats, kv, run):
+    rows, wide = kv.shape
+    each = qd.shape[0] // group
+    whole = pl.BlockSpec(memory_space=pltpu.VMEM)
+    dma = pltpu.SemaphoreType.DMA
+    return pl.pallas_call(
+        functools.partial(gather_kernel, group, cycle),
+        out_shape=(
+            jax.ShapeDtypeStruct((each, group, rows, wide), qd.dtype),
+            jax.ShapeDtypeStruct((group, each) + stats.shape[1:], stats.dtype),
+            jax.ShapeDtypeStruct((cycle * group, rows, wide), kv.dtype),
+            jax.ShapeDtypeStruct((cycle,) + run.shape, run.dtype),
+        ),
+        in_specs=[whole] * 4,
+        out_specs=(whole,) * 4,
+        scratch_shapes=[dma((4,))]
+        + [dma((group,))] * 6
+        + [dma((cycle,))] * 6,
+        compiler_params=pltpu.CompilerParams(
+            collective_id=0, has_side_effects=True, vmem_limit_bytes=40 * 1024 * 1024
+        ),
+    )(qd, stats, kv, run)
+
+
+def reduce_kernel(
+    group, cycle, dq_ref, dkv_ref, dq_out, dk_out, dv_out,
+    core_out, core_in, ring_out, ring_in, last, share,
+    own_sem, dq_send, dq_recv, core_send, core_recv, ring_send, ring_recv, end_send, end_recv,
+):
+    digits = digits_of(cycle)
+    levels = len(digits)
+    head, ctx = lax.axis_index("head"), lax.axis_index("ctx")
+    place = split_index(ctx, digits)
+    half = group // 2
+    each = dq_ref.shape[0]
+    width = dk_out.shape[1]
+    core, chip = lax.rem(head, 2), lax.div(head, 2)
+    sibling = head + 1 - 2 * core
+    ahead = [lax.rem(head + k, group) for k in range(group)]
+    behind = [lax.rem(head + group - k, group) for k in range(group)]
+
+    def moved(axis, k):
+        to = list(place)
+        to[axis] = lax.rem(place[axis] + k, digits[axis])
+        return join_index(to, digits)
+
+    greet(
+        [(h, ctx) for h in ahead[1:]]
+        + [(head, moved(axis, k)) for axis in range(levels) for k in range(1, digits[axis])]
+    )
+
+    def remote(src, dst, send, recv, to):
+        return pltpu.make_async_remote_copy(
+            src_ref=src, dst_ref=dst, send_sem=send, recv_sem=recv, device_id=to, device_id_type=MESH
+        )
+
+    started = []
+
+    def start(copy):
+        copy.start()
+        started.append(copy)
+
+    labels = [[]]
+    for size in digits:
+        labels = [label + [k] for label in labels for k in range(size)]
+    slot_of = lambda label: join_index(label, digits)
+
+    def level_of(label):
+        moving = [axis for axis in range(levels) if label[axis]]
+        return moving[-1] if moving else -1
+
+    labels.sort(key=lambda label: -level_of(label))
+
+    def terms(label, owner):
+        at = [lax.rem(p + o, n) for p, n, o in zip(place, digits, label)]
+        return dkv_ref[pl.ds(join_index(at, digits) * group + owner * half, half)]
+
+    for label in labels:
+        slot = slot_of(label)
+        core_out[slot] = terms(label, 1 - core).astype(jnp.bfloat16)
+        start(
+            remote(
+                core_out.at[slot], core_in.at[slot], core_send.at[slot], core_recv.at[slot], (sibling, ctx)
+            )
+        )
+    for k in range(1, group):
+        start(
+            remote(
+                dq_ref.at[:, ahead[k]],
+                dq_out.at[pl.ds(head * each, each)],
+                dq_send.at[k],
+                dq_recv.at[k],
+                (ahead[k], ctx),
+            )
+        )
+    own = pltpu.make_async_copy(dq_ref.at[:, head], dq_out.at[pl.ds(head * each, each)], own_sem.at[0])
+    own.start()
+
+    for label in labels:
+        slot = slot_of(label)
+        remote(
+            core_out.at[slot], core_in.at[slot], core_send.at[slot], core_recv.at[slot], (sibling, ctx)
+        ).wait_recv()
+        total = terms(label, core) + core_in[slot].astype(jnp.float32)
+        level = level_of(label)
+        for axis in range(levels - 1, level, -1):
+            for k in range(1, digits[axis]):
+                came = list(label)
+                came[axis] = k
+                at = slot_of(came)
+                remote(
+                    ring_out.at[at], ring_in.at[at], ring_send.at[at], ring_recv.at[at], (head, ctx)
+                ).wait_recv()
+                total = total + ring_in[at].astype(jnp.float32)
+        if level >= 0:
+            ring_out[slot] = total.astype(jnp.bfloat16)
+            to = (head, moved(level, label[level]))
+            start(remote(ring_out.at[slot], ring_in.at[slot], ring_send.at[slot], ring_recv.at[slot], to))
+        else:
+            share[...] = total
+
+    for j in range(half):
+        owner = core * half + j
+
+        @pl.when(owner != head)
+        def _():
+            remote(
+                share.at[j], last.at[chip], end_send.at[j], end_recv.at[chip], (owner, ctx)
+            ).start()
+
+        @pl.when(owner == head)
+        def _():
+            last[chip] = share[j]
+
+    my_half = lax.div(head, half)
+    for i in range(half):
+        source = i * 2 + my_half
+
+        @pl.when(source != head)
+        def _():
+            remote(
+                share.at[0], last.at[i], end_send.at[0], end_recv.at[i], (source, ctx)
+            ).wait_recv()
+
+    total = last[0]
+    for i in range(1, half):
+        total = total + last[i]
+    dk_out[...] = total[:, :width].astype(dk_out.dtype)
+    dv_out[...] = total[:, width:].astype(dv_out.dtype)
+
+    for k in range(1, group):
+        remote(
+            dq_ref.at[:, head],
+            dq_out.at[pl.ds(behind[k] * each, each)],
+            dq_send.at[k],
+            dq_recv.at[k],
+            (behind[k], ctx),
+        ).wait_recv()
+    own.wait()
+    for copy in started:
+        copy.wait_send()
+    for j in range(half):
+        owner = core * half + j
+
+        @pl.when(owner != head)
+        def _():
+            remote(
+                share.at[j], last.at[chip], end_send.at[j], end_recv.at[chip], (owner, ctx)
+            ).wait_send()
+
+
+def reduce_scatter(group, cycle, dq, dkv):
+    each, _, rows, width = dq.shape
+    wide = dkv.shape[2]
+    half = group // 2
+    whole = pl.BlockSpec(memory_space=pltpu.VMEM)
+    dma = pltpu.SemaphoreType.DMA
+    low = pltpu.VMEM((cycle, half, rows, wide), jnp.bfloat16)
+    return pl.pallas_call(
+        functools.partial(reduce_kernel, group, cycle),
+        out_shape=(
+            jax.ShapeDtypeStruct((each * group, rows, width), jnp.bfloat16),
+            jax.ShapeDtypeStruct((rows, width), jnp.bfloat16),
+            jax.ShapeDtypeStruct((rows, width), jnp.bfloat16),
+        ),
+        in_specs=[whole] * 2,
+        out_specs=(whole,) * 3,
+        scratch_shapes=[
+            low,
+            low,
+            low,
+            low,
+            pltpu.VMEM((half, rows, wide), jnp.float32),
+            pltpu.VMEM((half, rows, wide), jnp.float32),
+            dma((1,)),
+            dma((group,)),
+            dma((group,)),
+            dma((cycle,)),
+            dma((cycle,)),
+            dma((cycle,)),
+            dma((cycle,)),
+            dma((half,)),
+            dma((half,)),
+        ],
+        compiler_params=pltpu.CompilerParams(
+            collective_id=1, has_side_effects=True, vmem_limit_bytes=56 * 1024 * 1024
+        ),
+    )(dq, dkv)
+
+
 def local(queries, key_rows, value_rows, attn_output, grad_output, logsumexp, positions):
     cycle = lax.axis_size("ctx")
     group = lax.axis_size("head")
     width = queries.shape[2]
-    rows = positions.shape[0] * group
+    part = positions.shape[0]
+    rows = part * group
     run = rows // 2
     heads = queries.shape[0] // group
     row_delta = jnp.sum(grad_output.astype(jnp.float32) * attn_output.astype(jnp.float32), axis=2)
-    kv = lax.all_gather(
-        jnp.concatenate([key_rows, value_rows], axis=1), ("ctx", "head"), axis=0, tiled=True
+    kv = jnp.concatenate([key_rows, value_rows], axis=1)
+    qd = jnp.concatenate([queries, grad_output], axis=2)
+    stats = jnp.stack([logsumexp, row_delta], axis=1)
+    place = positions[0] // run
+    low_run = jnp.where(lax.axis_index("head") < group // 2, place, 2 * cycle - 1 - place)
+    qd, stats, kv, runs = gather(group, cycle, qd, stats, kv, jnp.full((8, 128), low_run, jnp.int32))
+    stats = stats.reshape(2, group // 2, heads, 2, part).transpose(3, 0, 2, 1, 4)
+    stats = stats.reshape(2, 2, 1, heads * run)
+    mine = lax.axis_index("ctx").reshape(1)
+    dq, dkv = tiles(
+        cycle,
+        runs[:, 0, 0],
+        mine,
+        qd.reshape(heads, rows, 2 * width),
+        stats[0],
+        stats[1],
+        kv.reshape(cycle * rows, 2 * width),
     )
-    places = lax.all_gather(positions, ("ctx", "head"), axis=0, tiled=True)
-    runs = places.reshape(cycle, rows)[:, 0] // run
-    mine = lax.axis_index("ctx").reshape(1)
-    qd = lax.all_to_all(
-        jnp.concatenate([queries, grad_output], axis=2), "head", split_axis=0, concat_axis=1, tiled=True
-    )
-    stats = lax.all_to_all(
-        jnp.stack([logsumexp, row_delta], axis=1), "head", split_axis=0, concat_axis=2, tiled=True
-    )
-    stats = stats.reshape(heads, 2, 2, run).transpose(1, 2, 0, 3).reshape(2, 2, 1, heads * run)
-    dq, dkv = tiles(cycle, runs, mine, qd, stats[0], stats[1], kv)
-    mine_kv = lax.psum_scatter(dkv, ("ctx", "head"), scatter_dimension=0, tiled=True)
-    grad_queries = lax.all_to_all(dq, "head", split_axis=1, concat_axis=0, tiled=True)
-    return (
-        grad_queries,
-        mine_kv[:, :width].astype(jnp.bfloat16),
-        mine_kv[:, width:].astype(jnp.bfloat16),
+    return reduce_scatter(
+        group,
+        cycle,
+        dq.reshape(heads, group, part, width),
+        dkv.reshape(cycle * group, part, 2 * width),
     )
 
 

time: 238 us -> 97.3 us (0.41)
  waiting for transfers between devices: 122 us -> 0 us
  Pallas kernels: 16.4 us -> 80 us
  blocking collectives: 62 us -> 0 us
  between operations: 14.1 us -> 3.29 us
  starting transfers between devices: 7.81 us -> 0 us
  other arithmetic: 8.78 us -> 4.38 us
  local copies, waits for them, and re-layouts: 5.9 us -> 8.33 us
    reduce_scatter x1 -> x0, waiting for transfers between devices: 120 us -> none  [local(): lax.psum_scatter(dkv, ('ctx', 'head'), scatter_dimension=0, tiled=True)]
    pallas_call x0 -> x2, Pallas kernels: none -> 63.6 us  [the longest x1 33.9 us: reduce_scatter(): pl.pallas_call(functools.partial(reduce_kernel, group, cycle), out_shape=...]
    all_gather x1 -> x0, blocking collectives: 47.7 us -> none  [local(): places = lax.all_gather(positions, ('ctx', 'head'), axis=0, tiled=True)]
    all_to_all x1 -> x0, blocking collectives: 14.3 us -> none  [local(): lax.all_to_all(dq, 'head', split_axis=1, concat_axis=0, tiled=True)]
    all_to_all x2 -> x0, starting transfers between devices: 7.73 us -> none  [the longest x1 4.21 us: local(): lax.all_to_all(jnp.stack([logsumexp, row_delta], axis=1), 'head', split_a...]
    unnamed x5 -> x7, local copies, waits for them, and re-layouts: 1.1 us -> 6.95 us
  transfers between devices with their start and end apart: 4 -> 0, of which waited for: 2 -> 0; matrix products, arithmetic and copies ran while one was open for 5% -> 0% of each run, Pallas kernels for 0% -> 0%
where the time goes in v2:
time: 97.3 us; the launch traced here: 96 us
  Pallas kernels  80 us (82%)
  local copies, waits for them, and re-layouts  8.33 us (9%)
  other arithmetic  4.38 us (5%)
  between operations  3.29 us (3%)
    pallas_call x1, Pallas kernels, reduce_scatter(): pl.pallas_call(functools.partial(reduce_kernel, group, cycle), out_shape=...  33.9 us
    pallas_call x1, Pallas kernels, gather(): pl.pallas_call(functools.partial(gather_kernel, group, cycle), out_shape=...  29.7 us
    pallas_call x1, Pallas kernels, tiles(): pl.pallas_call(functools.partial(tiles_kernel, cycle), out_shape=(jax.Sha...  16.4 us
    unnamed x7, local copies, waits for them, and re-layouts  6.95 us

profile of v2, /device:TPU:0, one launch (start us, length us, event | category | flops | bytes accessed | tf_op | source)
XLA Modules:
  0.0 96.0 jit_solution(17852315373134269142)
XLA Ops:
  3.2 1.5 %multiply_reduce_fusion = f32[16,128]{1,0:T(8,128)S(1)} fusion(bf16[16,128,128]{2,1,0:T(8,128)(2,1)} %param.10, bf16[16,128,128]{2,1,0:T(8,128)(2,1)} %param.11), kind=kLoop, calls=%fused_computation.1 | loop fusion | flops 1046528 | bytes 1056768 | tf_op jit(solution)/shard_map/reduce_sum | solution.py:454
  4.8 0.7 pad_maximum_fusion.2.stats_ref
  5.5 0.8 pad_maximum_fusion.1.kv_ref
  6.3 1.3 %pad_maximum_fusion.qd_ref = bf16[16,128,256]{2,1,0:T(8,128)(2,1)S(1)} fusion(bf16[16,128,128]{2,1,0:T(8,128)(2,1)} %param.11, bf16[16,128,128]{2,1,0:T(8,128)(2,1)} %param.7), kind=kLoop, calls=%fused_computation | loop fusion | flops 2097152 | bytes 2097152 | tf_op jit(solution)/shard_map/concatenate | solution.py:456
  7.6 29.7 %shard_map.94 = (bf16[4,4,128,256]{3,2,1,0:T(8,128)(2,1)S(1)}, f32[4,4,2,128]{3,2,1,0:T(2,128)S(1)}, bf16[32,128,256]{2,1,0:T(8,128)(2,1)S(1)}, s32[8,8,128]{2,1,0:T(8,128)S(1)}) custom-call(bf16[16,128,256]{2,1,0:T(8,128)(2,1)S(1)} %pad_maximum_fusion.qd_ref, f32[16,2,128]{2,1,0:T(2,128)S(1)} %pad_maximum_fusion.2.stats_ref, ...), custom_call_target="tpu_custom_call" | custom-call | tf_op jit(solution)/shard_map/pallas_call | solution.py:241
  37.4 0.0 copy-start
  37.4 1.3 %copy-done = bf16[32,128,256]{2,1,0:T(8,128)(2,1)} copy-done((bf16[32,128,256]{2,1,0:T(8,128)(2,1)}, bf16[32,128,256]{2,1,0:T(8,128)(2,1)S(1)}, u32[]{:S(2)}) %copy-start) | copy-done | bytes 2097176
  38.7 0.0 copy-start.1
  38.7 1.0 %copy-done.1 = bf16[4,4,128,256]{3,2,1,0:T(8,128)(2,1)} copy-done((bf16[4,4,128,256]{3,2,1,0:T(8,128)(2,1)}, bf16[4,4,128,256]{3,2,1,0:T(8,128)(2,1)S(1)}, u32[]{:S(2)}) %copy-start.1) | copy-done | bytes 1048600
  39.7 0.8 slice_reduce_fusion.runs_ref
  40.5 0.6 fusion
  41.1 16.4 %shard_map.95 = (bf16[4,512,128]{2,1,0:T(8,128)(2,1)}, f32[4096,256]{1,0:T(8,128)}) custom-call(s32[8]{0:T(128)} %slice_reduce_fusion.runs_ref, s32[1]{0:T(128)} %bitcast.3.mine_ref, bf16[4,512,256]{2,1,0:T(8,128)(2,1)} %bitcast.16, f32[2,1,1024]{2,1,0:T(1,128)} %bitcast.22, f32[2,1,1024]{2,1,0:T(1,128)} %bitcast.21, bf16[4096,256]{1,0:T(8,128)(2,1)} %bitcast.15), custom_call_target="tpu_custom_call" | custom-call | tf_op jit(solution)/shard_map/pallas_call | solution.py:79
  57.5 33.9 %shard_map.96 = (bf16[16,128,128]{2,1,0:T(8,128)(2,1)}, bf16[128,128]{1,0:T(8,128)(2,1)}, bf16[128,128]{1,0:T(8,128)(2,1)}) custom-call(bf16[4,4,128,128]{3,2,1,0:T(8,128)(2,1)} %bitcast.19, f32[32,128,256]{2,1,0:T(8,128)} %bitcast.18), custom_call_target="tpu_custom_call" | custom-call | tf_op jit(solution)/shard_map/pallas_call | solution.py:414
  91.4 1.9 %copy.17 = bf16[16,128,128]{2,1,0:T(8,128)(2,1)} copy(bf16[16,128,128]{2,1,0:T(8,128)(2,1)} %get-tuple-element.20) | data formatting | bytes 1048576
  93.3 1.4 %copy.18 = bf16[128,128]{1,0:T(8,128)(2,1)} copy(bf16[128,128]{1,0:T(8,128)(2,1)} %get-tuple-element.21) | data formatting | bytes 65536
  94.7 1.4 %copy.19 = bf16[128,128]{1,0:T(8,128)(2,1)} copy(bf16[128,128]{1,0:T(8,128)(2,1)} %get-tuple-element.22) | data formatting | bytes 65536
  (2 shorter events, 0.0 us)
Async XLA Ops:
  37.4 1.3 %copy-start = (bf16[32,128,256]{2,1,0:T(8,128)(2,1)}, bf16[32,128,256]{2,1,0:T(8,128)(2,1)S(1)}, u32[]{:S(2)}) copy-start(bf16[32,128,256]{2,1,0:T(8,128)(2,1)S(1)} %get-tuple-element.12) | copy-start | bytes 6291460
  38.7 1.0 %copy-start.1 = (bf16[4,4,128,256]{3,2,1,0:T(8,128)(2,1)}, bf16[4,4,128,256]{3,2,1,0:T(8,128)(2,1)S(1)}, u32[]{:S(2)}) copy-start(bf16[4,4,128,256]{3,2,1,0:T(8,128)(2,1)S(1)} %get-tuple-element.10) | copy-start | bytes 3145732

commit v3 on v2

--- a/solution.py
+++ b/solution.py
@@ -11,82 +11,6 @@
 
 def contract(a, b, axes):
     return lax.dot_general(a, b, (axes, ((), ())), preferred_element_type=jnp.float32)
-
-
-def tiles_kernel(cycle, runs_ref, mine_ref, qd_ref, lse_ref, delta_ref, kv_ref, dq_ref, dkv_ref, acc):
-    heads, rows, wide = qd_ref.shape
-    width = wide // 2
-    run = rows // 2
-    scaling = width ** (-0.5)
-    log2e = 1.0 / math.log(2.0)
-    me = mine_ref[0]
-    my_run = runs_ref[me]
-    acc[...] = jnp.zeros_like(acc)
-
-    def unit(query_half, key_row, diagonal):
-        rows_of = pl.ds(pl.multiple_of(query_half * run, run), run)
-        keys_of = pl.ds(pl.multiple_of(key_row, run), run)
-        query = qd_ref[:, rows_of, :width].reshape(heads * run, width)
-        grad = qd_ref[:, rows_of, width:].reshape(heads * run, width)
-        key = kv_ref[keys_of, :width]
-        value = kv_ref[keys_of, width:]
-        scores = contract(key, query, ((1,), (1,)))
-        prob = jnp.exp2(scores * (scaling * log2e) - lse_ref[query_half] * log2e)
-        if diagonal:
-            key_at = lax.broadcasted_iota(jnp.int32, scores.shape, 0)
-            query_at = lax.broadcasted_iota(jnp.int32, scores.shape, 1) % run
-            prob = jnp.where(key_at <= query_at, prob, 0.0)
-        grad_prob = contract(value, grad, ((1,), (1,)))
-        grad_score = (prob * (grad_prob - delta_ref[query_half])).astype(jnp.bfloat16)
-        value_grad = contract(prob.astype(jnp.bfloat16), grad, ((1,), (0,)))
-        key_grad = contract(grad_score, query, ((1,), (0,)))
-        acc[query_half] += contract(key.T, grad_score, ((1,), (0,)))
-        return keys_of, key_grad * scaling, value_grad
-
-    def put(terms):
-        keys_of, key_grad, value_grad = terms
-        dkv_ref[keys_of, :width] = key_grad
-        dkv_ref[keys_of, width:] = value_grad
-
-    def add(terms):
-        keys_of, key_grad, value_grad = terms
-        dkv_ref[keys_of, :width] += key_grad
-        dkv_ref[keys_of, width:] += value_grad
-
-    put(unit(1, me * rows, False))
-    add(unit(0, me * rows, True))
-    put(unit(1, me * rows + run, True))
-
-    @pl.loop(1, cycle)
-    def _(step):
-        other = lax.rem(me + step, cycle)
-        first = other * rows
-        late = (runs_ref[other] > my_run).astype(jnp.int32)
-        put(unit(1, first, False))
-        dkv_ref[pl.ds(pl.multiple_of(first + run, run), run), :] = jnp.zeros((run, wide), jnp.float32)
-        add(unit(late, first + late * run, False))
-
-    for half in range(2):
-        for head in range(heads):
-            part = acc[half, :, head * run : (head + 1) * run] * scaling
-            dq_ref[head, half * run : (half + 1) * run, :] = part.T.astype(jnp.bfloat16)
-
-
-def tiles(cycle, runs, mine, qd, lse, delta, kv):
-    heads, rows, wide = qd.shape
-    whole = pl.BlockSpec(memory_space=pltpu.VMEM)
-    scalars = pl.BlockSpec(memory_space=pltpu.SMEM)
-    return pl.pallas_call(
-        functools.partial(tiles_kernel, cycle),
-        out_shape=(
-            jax.ShapeDtypeStruct((heads, rows, wide // 2), jnp.bfloat16),
-            jax.ShapeDtypeStruct(kv.shape, jnp.float32),
-        ),
-        in_specs=[scalars, scalars, whole, whole, whole, whole],
-        out_specs=(whole, whole),
-        scratch_shapes=[pltpu.VMEM((2, wide // 2, heads * rows // 2), jnp.float32)],
-        compiler_params=pltpu.CompilerParams(vmem_limit_bytes=60 * 1024 * 1024),
-    )(runs, mine, qd, lse, delta, kv)
 
 
 MESH = pl.DeviceIdType.MESH
@@ -257,9 +181,9 @@
     )(qd, stats, kv, run)
 
 
-def reduce_kernel(
-    group, cycle, dq_ref, dkv_ref, dq_out, dk_out, dv_out,
-    core_out, core_in, ring_out, ring_in, last, share,
+def backward_kernel(
+    group, cycle, late_ref, qd_ref, lse_ref, delta_ref, kv_ref, dq_out, sums_out,
+    acc, pair, dq, own, core_out, core_in, ring_out, ring_in, last, share,
     own_sem, dq_send, dq_recv, core_send, core_recv, ring_send, ring_recv, end_send, end_recv,
 ):
     digits = digits_of(cycle)
@@ -267,8 +191,12 @@
     head, ctx = lax.axis_index("head"), lax.axis_index("ctx")
     place = split_index(ctx, digits)
     half = group // 2
-    each = dq_ref.shape[0]
-    width = dk_out.shape[1]
+    heads, rows, wide = qd_ref.shape
+    width = wide // 2
+    run = rows // 2
+    part = rows // group
+    scaling = width ** (-0.5)
+    log2e = 1.0 / math.log(2.0)
     core, chip = lax.rem(head, 2), lax.div(head, 2)
     sibling = head + 1 - 2 * core
     ahead = [lax.rem(head + k, group) for k in range(group)]
@@ -289,71 +217,171 @@
             src_ref=src, dst_ref=dst, send_sem=send, recv_sem=recv, device_id=to, device_id_type=MESH
         )
 
-    started = []
-
-    def start(copy):
-        copy.start()
-        started.append(copy)
-
-    labels = [[]]
-    for size in digits:
-        labels = [label + [k] for label in labels for k in range(size)]
-    slot_of = lambda label: join_index(label, digits)
-
-    def level_of(label):
-        moving = [axis for axis in range(levels) if label[axis]]
-        return moving[-1] if moving else -1
-
-    labels.sort(key=lambda label: -level_of(label))
-
-    def terms(label, owner):
-        at = [lax.rem(p + o, n) for p, n, o in zip(place, digits, label)]
-        return dkv_ref[pl.ds(join_index(at, digits) * group + owner * half, half)]
-
-    for label in labels:
-        slot = slot_of(label)
-        core_out[slot] = terms(label, 1 - core).astype(jnp.bfloat16)
-        start(
-            remote(
-                core_out.at[slot], core_in.at[slot], core_send.at[slot], core_recv.at[slot], (sibling, ctx)
+    acc[...] = jnp.zeros_like(acc)
+
+    def stats_of(ref, query_half, goes):
+        if query_half is not None:
+            return ref[query_half]
+        return jnp.where(goes, ref[1], ref[0])
+
+    def unit(query_half, first, key_half, diagonal, late=None):
+        def rows_of(at):
+            return slice(at * run, (at + 1) * run)
+
+        def keys_of(at):
+            return pl.ds(pl.multiple_of(first + at * run, run), run)
+
+        if late is None:
+            goes = None
+            query = qd_ref[:, rows_of(query_half), :width].reshape(heads * run, width)
+            grad = qd_ref[:, rows_of(query_half), width:].reshape(heads * run, width)
+            key = kv_ref[keys_of(key_half), :width]
+            value = kv_ref[keys_of(key_half), width:]
+        else:
+            goes = late > 0.5
+
+            def chosen(early_value, late_value):
+                flag = jnp.broadcast_to(late[:, :width], early_value.shape).astype(jnp.bfloat16)
+                return late_value * flag + early_value * (1 - flag)
+
+            query, grad = (
+                chosen(
+                    qd_ref[:, rows_of(0), columns].reshape(heads * run, width),
+                    qd_ref[:, rows_of(1), columns].reshape(heads * run, width),
+                )
+                for columns in (slice(0, width), slice(width, wide))
             )
+            key, value = (
+                chosen(kv_ref[keys_of(0), columns], kv_ref[keys_of(1), columns])
+                for columns in (slice(0, width), slice(width, wide))
+            )
+        scores = contract(key, query, ((1,), (1,)))
+        prob = jnp.exp2(scores * (scaling * log2e) - stats_of(lse_ref, query_half, goes) * log2e)
+        if diagonal:
+            key_at = lax.broadcasted_iota(jnp.int32, scores.shape, 0)
+            query_at = lax.broadcasted_iota(jnp.int32, scores.shape, 1) % run
+            prob = jnp.where(key_at <= query_at, prob, 0.0)
+        grad_prob = contract(value, grad, ((1,), (1,)))
+        grad_score = (prob * (grad_prob - stats_of(delta_ref, query_half, goes))).astype(jnp.bfloat16)
+        value_grad = contract(prob.astype(jnp.bfloat16), grad, ((1,), (0,)))
+        key_grad = contract(grad_score, query, ((1,), (0,)))
+        query_grad = contract(key.T, grad_score, ((1,), (0,)))
+        return query_grad, key_grad * scaling, value_grad
+
+    def by_owner(terms):
+        return terms.reshape(half, part, width)
+
+    def label_of(level, number):
+        label = [0] * levels
+        label[level] = lax.rem(number, digits[level] - 1) + 1
+        number = lax.div(number, digits[level] - 1)
+        for axis in range(level - 1, -1, -1):
+            label[axis] = lax.rem(number, digits[axis])
+            number = lax.div(number, digits[axis])
+        return label
+
+    def to_sibling(slot):
+        return remote(
+            core_out.at[slot], core_in.at[slot], core_send.at[slot], core_recv.at[slot], (sibling, ctx)
         )
-    for k in range(1, group):
-        start(
-            remote(
-                dq_ref.at[:, ahead[k]],
-                dq_out.at[pl.ds(head * each, each)],
-                dq_send.at[k],
-                dq_recv.at[k],
-                (ahead[k], ctx),
-            )
-        )
-    own = pltpu.make_async_copy(dq_ref.at[:, head], dq_out.at[pl.ds(head * each, each)], own_sem.at[0])
-    own.start()
-
-    for label in labels:
-        slot = slot_of(label)
-        remote(
-            core_out.at[slot], core_in.at[slot], core_send.at[slot], core_recv.at[slot], (sibling, ctx)
-        ).wait_recv()
-        total = terms(label, core) + core_in[slot].astype(jnp.float32)
-        level = level_of(label)
+
+    def hand_over(slot):
+        core_out[slot] = pair[1 - core].astype(jnp.bfloat16)
+        own[slot] = pair[core]
+        to_sibling(slot).start()
+
+    def along(slot, to):
+        return remote(ring_out.at[slot], ring_in.at[slot], ring_send.at[slot], ring_recv.at[slot], to)
+
+    def combined(label, level):
+        slot = join_index(label, digits)
+        to_sibling(slot).wait_recv()
+        total = own[slot] + core_in[slot].astype(jnp.float32)
         for axis in range(levels - 1, level, -1):
             for k in range(1, digits[axis]):
                 came = list(label)
                 came[axis] = k
-                at = slot_of(came)
-                remote(
-                    ring_out.at[at], ring_in.at[at], ring_send.at[at], ring_recv.at[at], (head, ctx)
-                ).wait_recv()
+                at = join_index(came, digits)
+                along(at, (head, ctx)).wait_recv()
                 total = total + ring_in[at].astype(jnp.float32)
-        if level >= 0:
-            ring_out[slot] = total.astype(jnp.bfloat16)
-            to = (head, moved(level, label[level]))
-            start(remote(ring_out.at[slot], ring_in.at[slot], ring_send.at[slot], ring_recv.at[slot], to))
-        else:
-            share[...] = total
-
+        return slot, total
+
+    def pass_on(label, level):
+        slot, total = combined(label, level)
+        ring_out[slot] = total.astype(jnp.bfloat16)
+        to = list(place)
+        to[level] = lax.rem(place[level] + label[level], digits[level])
+        along(slot, (head, join_index(to, digits))).start()
+
+    def count_of(level):
+        return math.prod(digits[:level]) * (digits[level] - 1)
+
+    for level in range(levels - 1, -1, -1):
+
+        @pl.loop(0, count_of(level))
+        def _(number):
+            label = label_of(level, number)
+            at = [lax.rem(p + o, n) for p, n, o in zip(place, digits, label)]
+            other = join_index(at, digits)
+            first = other * rows
+            late = late_ref[other]
+            query_grad, key_grad, value_grad = unit(1, first, 0, False)
+            acc[1] += query_grad
+            pair[0, :, :, :width] = by_owner(key_grad)
+            pair[0, :, :, width:] = by_owner(value_grad)
+            query_grad, key_grad, value_grad = unit(None, first, None, False, late)
+            goes = jnp.broadcast_to(late, query_grad.shape) > 0.5
+            acc[0] += jnp.where(goes, 0.0, query_grad)
+            acc[1] += jnp.where(goes, query_grad, 0.0)
+            goes = jnp.broadcast_to(late[:, :width], key_grad.shape) > 0.5
+            pair[0, :, :, :width] += by_owner(jnp.where(goes, 0.0, key_grad))
+            pair[0, :, :, width:] += by_owner(jnp.where(goes, 0.0, value_grad))
+            pair[1, :, :, :width] = by_owner(jnp.where(goes, key_grad, 0.0))
+            pair[1, :, :, width:] = by_owner(jnp.where(goes, value_grad, 0.0))
+            hand_over(join_index(label, digits))
+
+            @pl.when(number > 0)
+            def _():
+                pass_on(label_of(level, number - 1), level)
+
+            if level < levels - 1:
+
+                @pl.when(number == 0)
+                def _():
+                    pass_on(label_of(level + 1, count_of(level + 1) - 1), level + 1)
+
+    first = ctx * rows
+    query_grad, key_grad, value_grad = unit(1, first, 0, False)
+    acc[1] += query_grad
+    pair[0, :, :, :width] = by_owner(key_grad)
+    pair[0, :, :, width:] = by_owner(value_grad)
+    pass_on(label_of(0, count_of(0) - 1), 0)
+    query_grad, key_grad, value_grad = unit(0, first, 0, True)
+    acc[0] += query_grad
+    pair[0, :, :, :width] += by_owner(key_grad)
+    pair[0, :, :, width:] += by_owner(value_grad)
+    query_grad, key_grad, value_grad = unit(1, first, 1, True)
+    acc[1] += query_grad
+    pair[1, :, :, :width] = by_owner(key_grad)
+    pair[1, :, :, width:] = by_owner(value_grad)
+    hand_over(0)
+
+    for at in range(2):
+        for h in range(heads):
+            turned = (acc[at, :, h * run : (h + 1) * run] * scaling).T.astype(jnp.bfloat16)
+            dq[h, at * half : (at + 1) * half] = turned.reshape(half, part, width)
+
+    def query_copy(k, block, to):
+        return remote(
+            dq.at[:, block], dq_out.at[pl.ds(to[1] * heads, heads)], dq_send.at[k], dq_recv.at[k], (to[0], ctx)
+        )
+
+    for k in range(1, group):
+        query_copy(k, ahead[k], (ahead[k], head)).start()
+    stay = pltpu.make_async_copy(dq.at[:, head], dq_out.at[pl.ds(head * heads, heads)], own_sem.at[0])
+    stay.start()
+
+    share[...] = combined([0] * levels, -1)[1]
     for j in range(half):
         owner = core * half + j
 
@@ -380,20 +408,17 @@
     total = last[0]
     for i in range(1, half):
         total = total + last[i]
-    dk_out[...] = total[:, :width].astype(dk_out.dtype)
-    dv_out[...] = total[:, width:].astype(dv_out.dtype)
-
-    for k in range(1, group):
-        remote(
-            dq_ref.at[:, head],
-            dq_out.at[pl.ds(behind[k] * each, each)],
-            dq_send.at[k],
-            dq_recv.at[k],
-            (behind[k], ctx),
-        ).wait_recv()
-    own.wait()
-    for copy in started:
-        copy.wait_send()
+    sums_out[...] = total
+
+    for k in range(1, group):
+        query_copy(k, head, (behind[k], behind[k])).wait_recv()
+    stay.wait()
+    for k in range(1, group):
+        query_copy(k, ahead[k], (ahead[k], head)).wait_send()
+    for slot in range(cycle):
+        to_sibling(slot).wait_send()
+        if slot:
+            along(slot, (head, ctx)).wait_send()
     for j in range(half):
         owner = core * half + j
 
@@ -404,29 +429,34 @@
             ).wait_send()
 
 
-def reduce_scatter(group, cycle, dq, dkv):
-    each, _, rows, width = dq.shape
-    wide = dkv.shape[2]
+def backward(group, cycle, late, qd, lse, delta, kv):
+    heads, rows, wide = qd.shape
+    width = wide // 2
+    part = rows // group
     half = group // 2
     whole = pl.BlockSpec(memory_space=pltpu.VMEM)
     dma = pltpu.SemaphoreType.DMA
-    low = pltpu.VMEM((cycle, half, rows, wide), jnp.bfloat16)
+    low = pltpu.VMEM((cycle, half, part, wide), jnp.bfloat16)
+    ends = pltpu.VMEM((half, part, wide), jnp.float32)
     return pl.pallas_call(
-        functools.partial(reduce_kernel, group, cycle),
+        functools.partial(backward_kernel, group, cycle),
         out_shape=(
-            jax.ShapeDtypeStruct((each * group, rows, width), jnp.bfloat16),
-            jax.ShapeDtypeStruct((rows, width), jnp.bfloat16),
-            jax.ShapeDtypeStruct((rows, width), jnp.bfloat16),
+            jax.ShapeDtypeStruct((heads * group, part, width), jnp.bfloat16),
+            jax.ShapeDtypeStruct((part, wide), jnp.float32),
         ),
-        in_specs=[whole] * 2,
-        out_specs=(whole,) * 3,
+        in_specs=[whole] * 5,
+        out_specs=(whole,) * 2,
         scratch_shapes=[
+            pltpu.VMEM((2, width, heads * rows // 2), jnp.float32),
+            pltpu.VMEM((2, half, part, wide), jnp.float32),
+            pltpu.VMEM((heads, group, part, width), jnp.bfloat16),
+            pltpu.VMEM((cycle, half, part, wide), jnp.float32),
             low,
             low,
             low,
             low,
-            pltpu.VMEM((half, rows, wide), jnp.float32),
-            pltpu.VMEM((half, rows, wide), jnp.float32),
+            ends,
+            ends,
             dma((1,)),
             dma((group,)),
             dma((group,)),
@@ -438,9 +468,9 @@
             dma((half,)),
         ],
         compiler_params=pltpu.CompilerParams(
-            collective_id=1, has_side_effects=True, vmem_limit_bytes=56 * 1024 * 1024
+            collective_id=1, has_side_effects=True, vmem_limit_bytes=58 * 1024 * 1024
         ),
-    )(dq, dkv)
+    )(late, qd, lse, delta, kv)
 
 
 def local(queries, key_rows, value_rows, attn_output, grad_output, logsumexp, positions):
@@ -460,22 +490,19 @@
     qd, stats, kv, runs = gather(group, cycle, qd, stats, kv, jnp.full((8, 128), low_run, jnp.int32))
     stats = stats.reshape(2, group // 2, heads, 2, part).transpose(3, 0, 2, 1, 4)
     stats = stats.reshape(2, 2, 1, heads * run)
-    mine = lax.axis_index("ctx").reshape(1)
-    dq, dkv = tiles(
+    runs = runs[:, 0, 0]
+    late = (runs > low_run).astype(jnp.float32)
+    late = jnp.broadcast_to(late[:, None, None], (cycle, 1, heads * run))
+    grad_queries, sums = backward(
+        group,
         cycle,
-        runs[:, 0, 0],
-        mine,
+        late,
         qd.reshape(heads, rows, 2 * width),
         stats[0],
         stats[1],
         kv.reshape(cycle * rows, 2 * width),
     )
-    return reduce_scatter(
-        group,
-        cycle,
-        dq.reshape(heads, group, part, width),
-        dkv.reshape(cycle * group, part, 2 * width),
-    )
+    return grad_queries, sums[:, :width].astype(jnp.bfloat16), sums[:, width:].astype(jnp.bfloat16)
 
 
 def solution(mesh):

time: 97.3 us -> 81.2 us (0.83)
  Pallas kernels: 80 us -> 65.1 us
  local copies, waits for them, and re-layouts: 8.33 us -> 6.17 us
  other arithmetic: 4.38 us -> 5.44 us
    pallas_call x2 -> x1, Pallas kernels: 50.3 us -> 35.4 us  [backward(): pl.pallas_call(functools.partial(backward_kernel, group, cycle), out_shap...]
    unnamed x7 -> x5, local copies, waits for them, and re-layouts: 6.95 us -> 4.22 us
where the time goes in v3:
time: 81.2 us; the launch traced here: 80 us
  Pallas kernels  65.1 us (80%)
  local copies, waits for them, and re-layouts  6.17 us (8%)
  other arithmetic  5.44 us (7%)
  between operations  3.29 us (4%)
    pallas_call x1, Pallas kernels, backward(): pl.pallas_call(functools.partial(backward_kernel, group, cycle), out_shap...  35.4 us
    pallas_call x1, Pallas kernels, gather(): pl.pallas_call(functools.partial(gather_kernel, group, cycle), out_shape=...  29.7 us
    unnamed x5, local copies, waits for them, and re-layouts  4.22 us

profile of v3, /device:TPU:0, one launch (start us, length us, event | category | flops | bytes accessed | tf_op | source)
XLA Modules:
  0.0 80.0 jit_solution(1936884047957609885)
XLA Ops:
  3.2 1.5 %multiply_reduce_fusion = f32[16,128]{1,0:T(8,128)S(1)} fusion(bf16[16,128,128]{2,1,0:T(8,128)(2,1)} %param.10, bf16[16,128,128]{2,1,0:T(8,128)(2,1)} %param.11), kind=kLoop, calls=%fused_computation.1 | loop fusion | flops 1046528 | bytes 1056768 | tf_op jit(solution)/shard_map/reduce_sum | solution.py:484
  4.8 0.7 pad_maximum_fusion.2.stats_ref
  5.5 0.8 pad_maximum_fusion.1.kv_ref
  6.3 1.3 %pad_maximum_fusion.qd_ref = bf16[16,128,256]{2,1,0:T(8,128)(2,1)S(1)} fusion(bf16[16,128,128]{2,1,0:T(8,128)(2,1)} %param.11, bf16[16,128,128]{2,1,0:T(8,128)(2,1)} %param.7), kind=kLoop, calls=%fused_computation | loop fusion | flops 2097152 | bytes 2097152 | tf_op jit(solution)/shard_map/concatenate | solution.py:486
  7.6 29.7 %shard_map.94 = (bf16[4,4,128,256]{3,2,1,0:T(8,128)(2,1)S(1)}, f32[4,4,2,128]{3,2,1,0:T(2,128)S(1)}, bf16[32,128,256]{2,1,0:T(8,128)(2,1)S(1)}, s32[8,8,128]{2,1,0:T(8,128)S(1)}) custom-call(bf16[16,128,256]{2,1,0:T(8,128)(2,1)S(1)} %pad_maximum_fusion.qd_ref, f32[16,2,128]{2,1,0:T(2,128)S(1)} %pad_maximum_fusion.2.stats_ref, ...), custom_call_target="tpu_custom_call" | custom-call | tf_op jit(solution)/shard_map/pallas_call | solution.py:165
  37.4 0.0 copy-start
  37.4 1.3 %copy-done = bf16[32,128,256]{2,1,0:T(8,128)(2,1)} copy-done((bf16[32,128,256]{2,1,0:T(8,128)(2,1)}, bf16[32,128,256]{2,1,0:T(8,128)(2,1)S(1)}, u32[]{:S(2)}) %copy-start) | copy-done | bytes 2097176
  38.7 0.0 copy-start.1
  38.7 1.0 %copy-done.1 = bf16[4,4,128,256]{3,2,1,0:T(8,128)(2,1)} copy-done((bf16[4,4,128,256]{3,2,1,0:T(8,128)(2,1)}, bf16[4,4,128,256]{3,2,1,0:T(8,128)(2,1)S(1)}, u32[]{:S(2)}) %copy-start.1) | copy-done | bytes 1048600
  39.7 0.1 fusion
  39.9 0.6 fusion.2
  40.5 0.7 broadcast_in_dim.16.late_ref
  41.2 35.4 %shard_map.95 = (bf16[16,128,128]{2,1,0:T(8,128)(2,1)}, f32[128,256]{1,0:T(8,128)}) custom-call(f32[8,1,1024]{2,1,0:T(1,128)} %broadcast_in_dim.16.late_ref, bf16[4,512,256]{2,1,0:T(8,128)(2,1)} %bitcast.13, f32[2,1,1024]{2,1,0:T(1,128)} %bitcast.17, f32[2,1,1024]{2,1,0:T(1,128)} %bitcast.16, bf16[4096,256]{1,0:T(8,128)(2,1)} %bitcast.12), custom_call_target="tpu_custom_call" | custom-call | tf_op jit(solution)/shard_map/pallas_call | solution.py:441
  76.6 0.9 %convert.5 = bf16[128,256]{1,0:T(8,128)(2,1)S(1)} convert(f32[128,256]{1,0:T(8,128)} %get-tuple-element.14) | non-fusion elementwise | flops 32768 | bytes 196608 | tf_op jit(solution)/shard_map/convert.2
  77.5 0.6 fusion.1
  78.1 1.9 %copy.15 = bf16[16,128,128]{2,1,0:T(8,128)(2,1)} copy(bf16[16,128,128]{2,1,0:T(8,128)(2,1)} %get-tuple-element.22) | data formatting | bytes 1048576
  (2 shorter events, 0.0 us)
Async XLA Ops:
  37.4 1.3 %copy-start = (bf16[32,128,256]{2,1,0:T(8,128)(2,1)}, bf16[32,128,256]{2,1,0:T(8,128)(2,1)S(1)}, u32[]{:S(2)}) copy-start(bf16[32,128,256]{2,1,0:T(8,128)(2,1)S(1)} %get-tuple-element.12) | copy-start | bytes 6291460
  38.7 1.0 %copy-start.1 = (bf16[4,4,128,256]{3,2,1,0:T(8,128)(2,1)}, bf16[4,4,128,256]{3,2,1,0:T(8,128)(2,1)S(1)}, u32[]{:S(2)}) copy-start(bf16[4,4,128,256]{3,2,1,0:T(8,128)(2,1)S(1)} %get-tuple-element.10) | copy-start | bytes 3145732

commit v4 on v3

--- a/solution.py
+++ b/solution.py
@@ -43,7 +43,8 @@
 
 
 def gather_kernel(
-    group, cycle, qd_ref, stats_ref, kv_ref, run_ref, qd_out, stats_out, kv_out, run_out,
+    group, cycle, query_ref, grad_ref, output_ref, lse_ref, key_ref, value_ref, run_ref,
+    qd_out, stats_out, kv_out, run_out, stats_ref,
     own_sem, kv_send, kv_recv, qd_send, qd_recv, st_send, st_recv, run_send, run_recv,
     ring_send, ring_recv, core_send, core_recv,
 ):
@@ -51,7 +52,9 @@
     head, ctx = lax.axis_index("head"), lax.axis_index("ctx")
     place = split_index(ctx, digits)
     half = group // 2
-    each = qd_ref.shape[0] // group
+    each = query_ref.shape[0] // group
+    width = query_ref.shape[2]
+    columns = (slice(0, width), slice(width, 2 * width))
     core = lax.rem(head, 2)
     sibling = head + 1 - 2 * core
     ahead = [lax.rem(head + k, group) for k in range(group)]
@@ -72,28 +75,34 @@
         started.append(copy)
 
     for k in range(1, group):
-        start(remote(kv_ref, kv_out.at[ctx * group + head], kv_send.at[k], kv_recv.at[k], (ahead[k], ctx)))
+        for n, ref in enumerate((key_ref, value_ref)):
+            to = kv_out.at[ctx * group + head, :, columns[n]]
+            start(remote(ref, to, kv_send.at[n, k], kv_recv.at[n, k], (ahead[k], ctx)))
     for k in range(1, cycle):
         start(remote(run_ref, run_out.at[ctx], run_send.at[k], run_recv.at[k], (head, ctx_ahead[k])))
     for k in range(1, group):
         rows = pl.ds(ahead[k] * each, each)
-        start(remote(stats_ref.at[rows], stats_out.at[head], st_send.at[k], st_recv.at[k], (ahead[k], ctx)))
-        start(remote(qd_ref.at[rows], qd_out.at[:, head], qd_send.at[k], qd_recv.at[k], (ahead[k], ctx)))
+        for n, ref in enumerate((query_ref, grad_ref)):
+            to = qd_out.at[:, head, :, columns[n]]
+            start(remote(ref.at[rows], to, qd_send.at[n, k], qd_recv.at[n, k], (ahead[k], ctx)))
     mine = pl.ds(head * each, each)
+    here = kv_out.at[ctx * group + head]
     local_copies = [
-        pltpu.make_async_copy(kv_ref, kv_out.at[ctx * group + head], own_sem.at[0]),
-        pltpu.make_async_copy(run_ref, run_out.at[ctx], own_sem.at[1]),
-        pltpu.make_async_copy(stats_ref.at[mine], stats_out.at[head], own_sem.at[2]),
-        pltpu.make_async_copy(qd_ref.at[mine], qd_out.at[:, head], own_sem.at[3]),
+        pltpu.make_async_copy(key_ref, here.at[:, columns[0]], own_sem.at[0]),
+        pltpu.make_async_copy(value_ref, here.at[:, columns[1]], own_sem.at[1]),
+        pltpu.make_async_copy(run_ref, run_out.at[ctx], own_sem.at[2]),
+        pltpu.make_async_copy(query_ref.at[mine], qd_out.at[:, head, :, columns[0]], own_sem.at[3]),
+        pltpu.make_async_copy(grad_ref.at[mine], qd_out.at[:, head, :, columns[1]], own_sem.at[4]),
     ]
     for copy in local_copies:
         copy.start()
 
     local_copies[0].wait()
-    for k in range(1, group):
-        remote(
-            kv_ref, kv_out.at[ctx * group + behind[k]], kv_send.at[k], kv_recv.at[k], (behind[k], ctx)
-        ).wait_recv()
+    local_copies[1].wait()
+    for k in range(1, group):
+        for n, ref in enumerate((key_ref, value_ref)):
+            to = kv_out.at[ctx * group + behind[k], :, columns[n]]
+            remote(ref, to, kv_send.at[n, k], kv_recv.at[n, k], (behind[k], ctx)).wait_recv()
 
     def region(label, owner):
         at = [lax.rem(p + n - o, n) for p, n, o in zip(place, digits, label)]
@@ -117,6 +126,16 @@
 
     none = [0] * len(digits)
     forward(none, 0)
+    for h in range(query_ref.shape[0]):
+        product = grad_ref[h].astype(jnp.float32) * output_ref[h].astype(jnp.float32)
+        stats_ref[h, 0:1, :] = lse_ref[h : h + 1, :]
+        stats_ref[h, 1:2, :] = jnp.sum(product.T, axis=0, keepdims=True)
+    for k in range(1, group):
+        rows = pl.ds(ahead[k] * each, each)
+        start(remote(stats_ref.at[rows], stats_out.at[head], st_send.at[k], st_recv.at[k], (ahead[k], ctx)))
+    stay = pltpu.make_async_copy(stats_ref.at[mine], stats_out.at[head], own_sem.at[5])
+    stay.start()
+    local_copies.append(stay)
     labels = []
     held = [none]
     for axis in range(len(digits)):
@@ -148,37 +167,38 @@
         remote(
             stats_ref.at[mine], stats_out.at[behind[k]], st_send.at[k], st_recv.at[k], to
         ).wait_recv()
-        remote(
-            qd_ref.at[mine], qd_out.at[:, behind[k]], qd_send.at[k], qd_recv.at[k], to
-        ).wait_recv()
-    for copy in local_copies[1:]:
+        for n, ref in enumerate((query_ref, grad_ref)):
+            place_of = qd_out.at[:, behind[k], :, columns[n]]
+            remote(ref.at[mine], place_of, qd_send.at[n, k], qd_recv.at[n, k], to).wait_recv()
+    for copy in local_copies[2:]:
         copy.wait()
     for copy in started:
         copy.wait_send()
 
 
-def gather(group, cycle, qd, stats, kv, run):
-    rows, wide = kv.shape
-    each = qd.shape[0] // group
+def gather(group, cycle, queries, grads, outputs, lse, keys, values, run):
+    heads, rows, width = queries.shape
+    each, wide = heads // group, 2 * width
     whole = pl.BlockSpec(memory_space=pltpu.VMEM)
     dma = pltpu.SemaphoreType.DMA
     return pl.pallas_call(
         functools.partial(gather_kernel, group, cycle),
         out_shape=(
-            jax.ShapeDtypeStruct((each, group, rows, wide), qd.dtype),
-            jax.ShapeDtypeStruct((group, each) + stats.shape[1:], stats.dtype),
-            jax.ShapeDtypeStruct((cycle * group, rows, wide), kv.dtype),
+            jax.ShapeDtypeStruct((each, group, rows, wide), queries.dtype),
+            jax.ShapeDtypeStruct((group, each, 2, rows), jnp.float32),
+            jax.ShapeDtypeStruct((cycle * group, rows, wide), keys.dtype),
             jax.ShapeDtypeStruct((cycle,) + run.shape, run.dtype),
         ),
-        in_specs=[whole] * 4,
+        in_specs=[whole] * 7,
         out_specs=(whole,) * 4,
-        scratch_shapes=[dma((4,))]
-        + [dma((group,))] * 6
+        scratch_shapes=[pltpu.VMEM((heads, 2, rows), jnp.float32), dma((6,))]
+        + [dma((2, group))] * 4
+        + [dma((group,))] * 2
         + [dma((cycle,))] * 6,
         compiler_params=pltpu.CompilerParams(
             collective_id=0, has_side_effects=True, vmem_limit_bytes=40 * 1024 * 1024
         ),
-    )(qd, stats, kv, run)
+    )(queries, grads, outputs, lse, keys, values, run)
 
 
 def backward_kernel(
@@ -481,13 +501,19 @@
     rows = part * group
     run = rows // 2
     heads = queries.shape[0] // group
-    row_delta = jnp.sum(grad_output.astype(jnp.float32) * attn_output.astype(jnp.float32), axis=2)
-    kv = jnp.concatenate([key_rows, value_rows], axis=1)
-    qd = jnp.concatenate([queries, grad_output], axis=2)
-    stats = jnp.stack([logsumexp, row_delta], axis=1)
     place = positions[0] // run
     low_run = jnp.where(lax.axis_index("head") < group // 2, place, 2 * cycle - 1 - place)
-    qd, stats, kv, runs = gather(group, cycle, qd, stats, kv, jnp.full((8, 128), low_run, jnp.int32))
+    qd, stats, kv, runs = gather(
+        group,
+        cycle,
+        queries,
+        grad_output,
+        attn_output,
+        logsumexp,
+        key_rows,
+        value_rows,
+        jnp.full((8, 128), low_run, jnp.int32),
+    )
     stats = stats.reshape(2, group // 2, heads, 2, part).transpose(3, 0, 2, 1, 4)
     stats = stats.reshape(2, 2, 1, heads * run)
     runs = runs[:, 0, 0]

time: 81.2 us -> 82.3 us (1.014)
  local copies, waits for them, and re-layouts: 6.17 us -> 11.5 us
  other arithmetic: 5.44 us -> 1.06 us
    unnamed x5 -> x17, local copies, waits for them, and re-layouts: 4.22 us -> 9.52 us
    concatenate x2 -> x0, other arithmetic: 2.12 us -> none  [the longest x1 1.34 us: local(): qd = jnp.concatenate([queries, grad_output], axis=2)]
    reduce_sum x1 -> x0, other arithmetic: 1.55 us -> none  [local(): jnp.sum(grad_output.astype(jnp.float32) * attn_output.astype(jnp.float32)...]
where the time goes in v4:
time: 82.3 us; the launch traced here: 81 us
  Pallas kernels  65.2 us (79%)
  local copies, waits for them, and re-layouts  11.5 us (14%)
  between operations  3.29 us (4%)
  other arithmetic  1.06 us (1%)
    pallas_call x1, Pallas kernels, backward(): pl.pallas_call(functools.partial(backward_kernel, group, cycle), out_shap...  35.4 us
    pallas_call x1, Pallas kernels, gather(): pl.pallas_call(functools.partial(gather_kernel, group, cycle), out_shape=...  29.8 us
    unnamed x17, local copies, waits for them, and re-layouts  9.52 us

profile of v4, /device:TPU:0, one launch (start us, length us, event | category | flops | bytes accessed | tf_op | source)
XLA Modules:
  0.0 81.0 jit_solution(17094435817851205627)
XLA Ops:
  3.2 0.0 copy-start.2
  3.3 1.0 %copy-done.2 = bf16[16,128,128]{2,1,0:T(8,128)(2,1)S(1)} copy-done((bf16[16,128,128]{2,1,0:T(8,128)(2,1)S(1)}, bf16[16,128,128]{2,1,0:T(8,128)(2,1)}, u32[]{:S(2)}) %copy-start.2) | copy-done | bytes 524312
  4.3 0.0 copy-start.3
  4.3 1.0 %copy-done.3 = bf16[16,128,128]{2,1,0:T(8,128)(2,1)S(1)} copy-done((bf16[16,128,128]{2,1,0:T(8,128)(2,1)S(1)}, bf16[16,128,128]{2,1,0:T(8,128)(2,1)}, u32[]{:S(2)}) %copy-start.3) | copy-done | bytes 524312
  5.3 0.0 copy-start.4
  5.3 1.0 %copy-done.4 = bf16[16,128,128]{2,1,0:T(8,128)(2,1)S(1)} copy-done((bf16[16,128,128]{2,1,0:T(8,128)(2,1)S(1)}, bf16[16,128,128]{2,1,0:T(8,128)(2,1)}, u32[]{:S(2)}) %copy-start.4) | copy-done | bytes 524312
  6.4 0.0 copy-start.5
  6.4 0.8 copy-done.5
  7.1 0.0 copy-start.6
  7.1 0.8 copy-done.6
  7.9 0.0 copy-start.7
  7.9 0.7 copy-done.7
  8.6 29.8 %shard_map.94 = (bf16[4,4,128,256]{3,2,1,0:T(8,128)(2,1)S(1)}, f32[4,4,2,128]{3,2,1,0:T(2,128)S(1)}, bf16[32,128,256]{2,1,0:T(8,128)(2,1)S(1)}, s32[8,8,128]{2,1,0:T(8,128)S(1)}) custom-call(bf16[16,128,128]{2,1,0:T(8,128)(2,1)S(1)} %copy-done.2, bf16[16,128,128]{2,1,0:T(8,128)(2,1)S(1)} %copy-done.3, bf16[16,128,128]{2,1,0:T(8,128)(2,1)S(1)} %copy-done.4, ...), custom_call_target="tpu_custom_call" | custom-call | tf_op jit(solution)/shard_map/pallas_call | solution.py:184
  38.4 0.0 copy-start
  38.4 1.3 %copy-done = bf16[32,128,256]{2,1,0:T(8,128)(2,1)} copy-done((bf16[32,128,256]{2,1,0:T(8,128)(2,1)}, bf16[32,128,256]{2,1,0:T(8,128)(2,1)S(1)}, u32[]{:S(2)}) %copy-start) | copy-done | bytes 2097176
  39.7 0.0 copy-start.1
  39.7 1.0 %copy-done.1 = bf16[4,4,128,256]{3,2,1,0:T(8,128)(2,1)} copy-done((bf16[4,4,128,256]{3,2,1,0:T(8,128)(2,1)}, bf16[4,4,128,256]{3,2,1,0:T(8,128)(2,1)S(1)}, u32[]{:S(2)}) %copy-start.1) | copy-done | bytes 1048600
  40.7 0.1 fusion
  40.9 0.6 fusion.2
  41.5 0.7 broadcast_in_dim.16.late_ref
  42.2 35.4 %shard_map.95 = (bf16[16,128,128]{2,1,0:T(8,128)(2,1)}, f32[128,256]{1,0:T(8,128)}) custom-call(f32[8,1,1024]{2,1,0:T(1,128)} %broadcast_in_dim.16.late_ref, bf16[4,512,256]{2,1,0:T(8,128)(2,1)} %bitcast.11, f32[2,1,1024]{2,1,0:T(1,128)} %bitcast.15, f32[2,1,1024]{2,1,0:T(1,128)} %bitcast.14, bf16[4096,256]{1,0:T(8,128)(2,1)} %bitcast.10), custom_call_target="tpu_custom_call" | custom-call | tf_op jit(solution)/shard_map/pallas_call | solution.py:461
  77.6 0.9 %convert.5 = bf16[128,256]{1,0:T(8,128)(2,1)S(1)} convert(f32[128,256]{1,0:T(8,128)} %get-tuple-element.14) | non-fusion elementwise | flops 32768 | bytes 196608 | tf_op jit(solution)/shard_map/convert.2
  78.5 0.6 fusion.1
  79.1 1.9 %copy.15 = bf16[16,128,128]{2,1,0:T(8,128)(2,1)} copy(bf16[16,128,128]{2,1,0:T(8,128)(2,1)} %get-tuple-element.22) | data formatting | bytes 1048576
  (2 shorter events, 0.0 us)
Async XLA Ops:
  3.2 1.0 %copy-start.2 = (bf16[16,128,128]{2,1,0:T(8,128)(2,1)S(1)}, bf16[16,128,128]{2,1,0:T(8,128)(2,1)}, u32[]{:S(2)}) copy-start(bf16[16,128,128]{2,1,0:T(8,128)(2,1)} %query_ref.1) | copy-start | bytes 1572868
  4.3 1.0 %copy-start.3 = (bf16[16,128,128]{2,1,0:T(8,128)(2,1)S(1)}, bf16[16,128,128]{2,1,0:T(8,128)(2,1)}, u32[]{:S(2)}) copy-start(bf16[16,128,128]{2,1,0:T(8,128)(2,1)} %grad_ref.1) | copy-start | bytes 1572868
  5.3 1.0 %copy-start.4 = (bf16[16,128,128]{2,1,0:T(8,128)(2,1)S(1)}, bf16[16,128,128]{2,1,0:T(8,128)(2,1)}, u32[]{:S(2)}) copy-start(bf16[16,128,128]{2,1,0:T(8,128)(2,1)} %output_ref.1) | copy-start | bytes 1572868
  6.4 0.8 copy-start.5
  7.1 0.8 copy-start.6
  7.9 0.7 copy-start.7
  38.4 1.3 %copy-start = (bf16[32,128,256]{2,1,0:T(8,128)(2,1)}, bf16[32,128,256]{2,1,0:T(8,128)(2,1)S(1)}, u32[]{:S(2)}) copy-start(bf16[32,128,256]{2,1,0:T(8,128)(2,1)S(1)} %get-tuple-element.12) | copy-start | bytes 6291460
  39.7 1.0 %copy-start.1 = (bf16[4,4,128,256]{3,2,1,0:T(8,128)(2,1)}, bf16[4,4,128,256]{3,2,1,0:T(8,128)(2,1)S(1)}, u32[]{:S(2)}) copy-start(bf16[4,4,128,256]{3,2,1,0:T(8,128)(2,1)S(1)} %get-tuple-element.10) | copy-start | bytes 3145732
